TPU v7x, 256 devices: a whole 4x4x8 slice. The times are simulated.
256 devices in a mesh: blk: 32 (over z, y_hi, core), uly: 8 (over x, y_lo).
Axes of the slice: x: 4, y: 4 (y_hi: 2, y_lo: 2; y = y_hi * 2 + y_lo), z: 8, core: 2. Of those that a mesh axis runs over, the one named last changes fastest.
Arguments:
- frames: bfloat16 [256, 64, 1152], P('blk', 'uly'), may hold values from -6 to 6
- vis_gain: float32 [1152], replicated, may hold values from 0.25 to 1.75
- proj_weight: bfloat16 [1152, 3584], P(None, 'uly'), may hold values from -0.1875 to 0.1875
- text_embed: bfloat16 [16384, 3584], P('blk', 'uly'), may hold values from -6 to 6
- text_lengths: int32 [32, 5], P('blk'), may hold values from 1 to 256, 512 in all within a row
- norm_gain: float32 [3584], P('uly'), may hold values from 0.25 to 1.75
- q_weight: bfloat16 [3584, 2048], P('uly'), as said below
- k_weight: bfloat16 [3584, 512], P('uly'), as said below
- v_weight: bfloat16 [3584, 512], P('uly'), may hold values from -0.09375 to 0.09375
- q_bias: float32 [2048], replicated, may hold values from -4 to 4
- k_bias: float32 [512], replicated, may hold values from -4 to 4
- v_bias: float32 [512], replicated, may hold values from -4 to 4
Outputs:
- attended: bfloat16 [24576, 2048], P('blk', 'uly')
Inputs may be any that keep to these rules, and one draw needn't show every extreme that they name: `text_lengths`: row b gives the lengths of the text runs of group b, the first before its first pooled frame and the last after its last; each row sums to 512. `q_weight`: entries of order 3584 ** -0.5. `k_weight`: entries of order 3584 ** -0.5.
All inputs are finite; a program needn't handle non-finite values.
Results may differ from a plain program's by a relative error of at most 0.006.
Values may be sent and summed in bfloat16 or wider, within the bound.
A program may use at most 64 MiB of HBM per device.

v0:
```python
import math

import jax
import jax.numpy as jnp
from jax import lax
from jax.sharding import PartitionSpec as P

PATCH = 64
D = 3584
HQ = 16
KVH = 4
HD = 128


def from_behind(value, axis, steps):
    count = lax.axis_size(axis)
    first, last = (max(0, -steps), min(count, count - steps))
    return lax.ppermute(value, axis, [(source, source + steps) for source in range(first, last)])


def pool_frames(frames, tail_frames):
    extended = jnp.concatenate([frames, tail_frames], 0).astype(jnp.float32)
    paired_frame_sums = extended.reshape((extended.shape[0] // 2, 2) + extended.shape[1:]).sum(1)
    return (paired_frame_sums[:-1] + paired_frame_sums[1:]) * 0.25


def layer_norm(values_in, gain_vec):
    average = jnp.mean(values_in, -1, keepdims=True)
    centred = values_in - average
    variance = jnp.mean(centred * centred, -1, keepdims=True)
    return centred * lax.rsqrt(variance + 1e-06) * gain_vec


def alternate(vis_rows, text_rows, run_lengths, patch_len):
    frame_count = run_lengths.shape[0] - 1
    seq_total = vis_rows.shape[0] + text_rows.shape[0]
    run_ends = jnp.cumsum(run_lengths[:frame_count])
    starts = run_ends + patch_len * jnp.arange(frame_count, dtype=jnp.int32)
    positions = jnp.arange(seq_total, dtype=jnp.int32)[:, None]
    inside = (positions >= starts[None]) & (positions < starts[None] + patch_len)
    before = (positions >= starts[None] + patch_len).astype(jnp.int32)
    frame_ids = jnp.arange(frame_count, dtype=jnp.int32)[None]
    vis_index = jnp.sum(jnp.where(inside, frame_ids * patch_len + positions - starts[None], 0), 1)
    text_index = jnp.clip(
        positions[:, 0] - patch_len * jnp.sum(before, 1), 0, text_rows.shape[0] - 1
    )
    in_vision = jnp.any(inside, 1)
    return jnp.where(
        in_vision[:, None], jnp.take(vis_rows, vis_index, 0), jnp.take(text_rows, text_index, 0)
    )


def rotate(vectors, positions):
    half_dim = vectors.shape[-1] // 2
    inv_freq = jnp.power(
        jnp.float32(1000000.0), -jnp.arange(half_dim, dtype=jnp.float32) * (2.0 / vectors.shape[-1])
    )
    angles = positions.astype(jnp.float32)[:, None] * inv_freq[None]
    cosine = jnp.cos(angles)[:, None, :]
    sine = jnp.sin(angles)[:, None, :]
    first = vectors[..., :half_dim]
    second = vectors[..., half_dim:]
    return jnp.concatenate([first * cosine - second * sine, second * cosine + first * sine], -1)


def shards(
    frames,
    vis_gain,
    proj_weight,
    text_embed,
    text_lengths,
    norm_gain,
    q_weight,
    k_weight,
    v_weight,
    q_bias,
    k_bias,
    v_bias,
):
    uly_count = lax.axis_size("uly")
    slot_index = lax.axis_index("uly")
    group_index = lax.axis_index("blk")
    halo_frames = from_behind(frames[:2], "blk", -1)
    pooled = pool_frames(frames, halo_frames)
    normal_vis = layer_norm(pooled, vis_gain).astype(jnp.bfloat16)
    vis_rows = jnp.einsum(
        "fpv,vd->fpd",
        lax.all_gather(normal_vis, "uly", axis=1, tiled=True),
        proj_weight,
        preferred_element_type=jnp.float32,
    ).astype(jnp.bfloat16)
    vis_rows = vis_rows.reshape(-1, vis_rows.shape[-1])
    sequence = alternate(vis_rows, text_embed, text_lengths[0], PATCH)
    seq_float = sequence.astype(jnp.float32)
    row_sums = lax.psum(jnp.sum(seq_float * seq_float, 1), "uly")
    normalized_rows = (seq_float * lax.rsqrt(row_sums[:, None] / D + 1e-06) * norm_gain).astype(
        jnp.bfloat16
    )
    q_dev = HQ // uly_count
    group_size = HQ // KVH
    kv_dev = max(1, q_dev // group_size)
    repeat_count = max(1, group_size // q_dev)
    local_rows = q_weight.shape[0]
    slot_q = q_weight.reshape(local_rows, uly_count, q_dev * HD)
    slot_k = jnp.repeat(k_weight.reshape(local_rows, KVH, HD), repeat_count, axis=1)
    slot_v = jnp.repeat(v_weight.reshape(local_rows, KVH, HD), repeat_count, axis=1)
    slot_weight_matrix = jnp.concatenate([slot_q, slot_k, slot_v], 2)
    bias_q = q_bias.reshape(uly_count, q_dev * HD)
    bias_k = jnp.repeat(k_bias.reshape(KVH, HD), repeat_count, axis=0)
    bias_v = jnp.repeat(v_bias.reshape(KVH, HD), repeat_count, axis=0)
    slot_bias = lax.dynamic_index_in_dim(
        jnp.concatenate([bias_q, bias_k, bias_v], 1), slot_index, 0, keepdims=False
    )
    seq_rows = normalized_rows.shape[0]
    projected = lax.psum_scatter(
        jnp.einsum(
            "wt,tai->awi", normalized_rows, slot_weight_matrix, preferred_element_type=jnp.float32
        ),
        "uly",
        scatter_dimension=0,
        tiled=True,
    )[0]
    projected = projected + slot_bias
    positions = group_index * seq_rows + jnp.arange(seq_rows, dtype=jnp.int32)
    q_cols = q_dev * HD
    kv_cols = kv_dev * HD
    queries = rotate(projected[:, :q_cols].reshape(seq_rows, q_dev, HD), positions).astype(
        jnp.bfloat16
    )
    keys = rotate(
        projected[:, q_cols : q_cols + kv_cols].reshape(seq_rows, kv_dev, HD), positions
    ).astype(jnp.bfloat16)
    values = projected[:, q_cols + kv_cols :].reshape(seq_rows, kv_dev, HD).astype(jnp.bfloat16)
    per_group = q_dev // kv_dev
    query_groups = queries.reshape(seq_rows, kv_dev, per_group, HD)
    last_position = positions[-1]

    def block_attention_step(state, block_data):
        key_block, value_tile_block, key_start = block_data

        def compute(old_state):
            top_score, denoms, accum = old_state
            scores = jnp.einsum(
                "qkgd,skd->kgqs", query_groups, key_block, preferred_element_type=jnp.float32
            ) / math.sqrt(HD)
            key_position_list = key_start + jnp.arange(key_block.shape[0], dtype=jnp.int32)
            allowed = key_position_list[None, None, None, :] <= positions[None, None, :, None]
            new_top = jnp.maximum(top_score, jnp.max(jnp.where(allowed, scores, -1e30), -1))
            weights = jnp.where(allowed, jnp.exp(scores - new_top[..., None]), 0.0)
            rescale = jnp.exp(top_score - new_top)
            denoms = denoms * rescale + jnp.sum(weights, -1)
            accum = accum * rescale[..., None] + jnp.einsum(
                "kgqs,skd->kgqd",
                weights.astype(jnp.bfloat16),
                value_tile_block,
                preferred_element_type=jnp.float32,
            )
            return (new_top, denoms, accum)

        return (
            lax.cond(key_start <= last_position, compute, lambda unchanged: unchanged, state),
            None,
        )

    initial = (
        jnp.full((kv_dev, per_group, seq_rows), -1e30, jnp.float32),
        jnp.zeros((kv_dev, per_group, seq_rows), jnp.float32),
        jnp.zeros((kv_dev, per_group, seq_rows, HD), jnp.float32),
    )
    state = initial
    key_piece = lax.all_gather(keys, "blk", axis=0, tiled=True)
    value_piece = lax.all_gather(values, "blk", axis=0, tiled=True)
    block_count = key_piece.shape[0] // seq_rows
    block_data = (
        key_piece.reshape(block_count, seq_rows, kv_dev, HD),
        value_piece.reshape(block_count, seq_rows, kv_dev, HD),
        seq_rows * jnp.arange(block_count, dtype=jnp.int32),
    )
    state, unused = lax.scan(block_attention_step, state, block_data)
    top_score, denoms, accum = state
    result = accum / denoms[..., None]
    return jnp.transpose(result, (2, 0, 1, 3)).reshape(seq_rows, q_cols).astype(jnp.bfloat16)


def solution(mesh):
    placed = (
        P("blk", "uly", None),
        P(),
        P(None, "uly"),
        P("blk", "uly"),
        P("blk", None),
        P("uly"),
        P("uly", None),
        P("uly", None),
        P("uly", None),
        P(),
        P(),
        P(),
    )
    return jax.shard_map(
        shards, mesh=mesh, in_specs=placed, out_specs=P("blk", "uly"), check_vma=False
    )
```

profile of v0, /device:TPU:249, one launch (start us, length us, event | category | flops | bytes accessed | tf_op | source)
XLA Modules:
  0.0 814.7 jit_solution(8522547271068737094)
XLA Ops:
  7.4 2.6 collective-permute-start
  14.6 2.9 copy.60
  17.5 2.7 gather_fusion.1
  20.7 23.8 %all_gather.9 = bf16[4,64,1152]{2,1,0:T(8,128)(2,1)S(1)} all-gather(bf16[4,8,1152]{2,1,0:T(8,128)(2,1)S(1)} %multiply_convert_fusion), channel_id=1, replica_groups=mesh['blk'=32,'uly'=8] {'uly'}, dimensions={1}, use_global_device_ids=true | all-gather | bytes 663552 | tf_op jit(solution)/shard_map/all_gather | solution.py:88
  45.0 2.7 gather_fusion
  49.3 12.4 %psum.7 = f32[768]{0:T(1024)S(1)} all-reduce(f32[768]{0:T(1024)S(1)} %get-tuple-element.226), channel_id=1, replica_groups=mesh['blk'=32,'uly'=8] {'uly'}, use_global_device_ids=true, to_apply=%region_8.9 | all-reduce | flops 768 | bytes 6144 | tf_op jit(solution)/shard_map/psum | solution.py:95
  62.0 10.0 %convolution_bitcast_fusion = f32[8,768,512]{1,2,0:T(8,128)} fusion(bf16[448,8,128]{2,0,1:T(8,128)(2,1)S(1)} %bitcast.131, bf16[448,8,128]{2,0,1:T(8,128)(2,1)S(1)} %bitcast.130, bf16[448,8,256]{2,0,1:T(8,128)(2,1)} %bitcast.128, bf16[768,448]{1,0:T(8,128)(2,1)} %get-tuple-element.227, f32[448]{0:T(512)S(1)} %copy-done.7, f32[768]{0:T(1024)S(1)} %add_rsqrt_fusion), kind=kOutput, calls=%fused_computation.32 | convolution fusion | flops 2830958592 | bytes 16945920 | tf_op jit(solution)/shard_map/wt,tai->awi/dot_general | solution.py:116
  72.8 259.7 %reduce-scatter.2.cloned.1.call-done = f32[1,768,512]{1,2,0:T(8,128)} async-done(((f32[8,768,512]{1,2,0:T(8,128)}), f32[1,768,512]{1,2,0:T(8,128)}) %reduce-scatter.2.cloned.1.call-update) | async-done | bytes 1572880 | tf_op jit(solution)/shard_map/reduce_scatter | solution.py:115
  339.8 89.5 %all-gather.4.cloned.1.call-done = bf16[24576,1,128]{0,2,1:T(8,128)(2,1)} async-done(((bf16[768,1,128]{0,2,1:T(8,128)(2,1)}), bf16[24576,1,128]{0,2,1:T(8,128)(2,1)}) %all-gather.4.cloned.1.call-update) | async-done | bytes 6291472 | tf_op jit(solution)/shard_map/all_gather | solution.py:171
  429.3 8.7 %copy.48 = bf16[24576,1,128]{2,0,1:T(8,128)(2,1)} copy(bf16[24576,1,128]{0,2,1:T(8,128)(2,1)} %all-gather.4.cloned.1.call-done) | data formatting | bytes 12582912
  437.9 85.0 %all-gather.6.cloned.1.call-done = bf16[24576,128]{0,1:T(8,128)(2,1)} async-done(((bf16[768,128]{0,1:T(8,128)(2,1)}), bf16[24576,128]{0,1:T(8,128)(2,1)}) %all-gather.6.cloned.1.call-update) | async-done | bytes 6291472 | tf_op jit(solution)/shard_map/all_gather | solution.py:172
  522.9 8.6 %copy.49 = bf16[24576,128]{1,0:T(8,128)(2,1)} copy(bf16[24576,128]{0,1:T(8,128)(2,1)} %all-gather.6.cloned.1.call-done) | data formatting | bytes 12582912
  531.6 275.0 %while.15 = (s32[]{:T(128)}, f32[1,2,768]{2,1,0:T(2,128)S(1)}, f32[1,2,768]{2,1,0:T(2,128)S(1)}, f32[1,2,768,128]{3,2,1,0:T(8,128)S(1)}, s32[32]{0:T(128)S(1)}, ...) while((s32[]{:T(128)}, f32[1,2,768]{2,1,0:T(2,128)S(1)}, ...), condition=%wide.region_15.16_spmd.clone, body=%wide.region_10.15_spmd.clone.sunk | while | flops 617945088 | bytes 18992408 | solution.py:179
  533.5 6.7 conditional.3
  542.1 6.7 conditional.3
  550.7 6.7 conditional.3
  559.3 6.7 conditional.3
  567.9 6.7 conditional.3
  576.5 6.7 conditional.3
  579.5 2.5 fusion.14
  585.1 6.7 conditional.3
  593.6 6.7 conditional.3
  602.2 6.7 conditional.3
  610.8 6.7 conditional.3
  613.9 2.5 fusion.14
  619.4 6.7 conditional.3
  628.0 6.7 conditional.3
  636.6 6.7 conditional.3
  645.2 6.7 conditional.3
  648.3 2.5 fusion.14
  653.8 6.7 conditional.3
  662.4 6.7 conditional.3
  671.0 6.7 conditional.3
  679.6 6.7 conditional.3
  688.2 6.7 conditional.3
  696.8 6.7 conditional.3
  705.4 6.7 conditional.3
  714.0 6.7 conditional.3
  722.6 6.7 conditional.3
  731.1 6.7 conditional.3
  739.7 6.7 conditional.3
  748.3 6.7 conditional.3
  756.9 6.7 conditional.3
  765.5 6.7 conditional.3
  774.1 6.7 conditional.3
  782.7 6.7 conditional.3
  791.3 6.7 conditional.3
  799.9 6.7 conditional.3
  (395 shorter events, 241.6 us)
Async XLA Ops:
  6.5 37.9 %copy-start = (bf16[1152,448]{0,1:T(8,128)(2,1)S(1)}, bf16[1152,448]{0,1:T(8,128)(2,1)}, u32[]{:S(2)}) copy-start(bf16[1152,448]{0,1:T(8,128)(2,1)} %param.18) | copy-start | bytes 3096580
  6.5 325.9 %reduce-scatter.2.cloned.1.call-start = ((), (), s32[]{:S(2)}) async-start(), calls=%async_computation.1 | async-start | bytes 14155776 | tf_op jit(solution)/shard_map/reduce_scatter | solution.py:115
  7.4 12.8 %collective-permute-start = (bf16[2,8,1152]{2,1,0:T(8,128)(2,1)S(1)}, bf16[2,8,1152]{2,1,0:T(8,128)(2,1)S(1)}, u32[]{:S(2)}, u32[]{:S(2)}) collective-permute-start(bf16[2,8,1152]{2,1,0:T(8,128)(2,1)S(1)} %slice.40), channel_id=1, source_target_pairs={{8,0},{16,8},{24,16},{32,24},{40,32},{48,40},{56,48},{64,56},{72,6... | collective-permute-start | bytes 110600 | tf_op jit(solution)/shard_map/ppermute | solution.py:18
  14.6 5.6 copy-start.2
  17.5 3.1 copy-start.3
  44.9 17.0 %copy-start.7 = (f32[448]{0:T(512)S(1)}, f32[448]{0:T(512)}, u32[]{:S(2)}) copy-start(f32[448]{0:T(512)} %param.21) | copy-start | bytes 5380
  72.0 0.7 copy-start.4
  72.0 0.7 copy-start.5
  72.0 0.7 copy-start.6
  72.0 357.3 %all-gather.4.cloned.1.call-start = ((), (), s32[]{:S(2)}) async-start(), calls=%async_computation.2 | async-start | bytes 6488064 | tf_op jit(solution)/shard_map/all_gather | solution.py:171
  335.6 187.3 %all-gather.6.cloned.1.call-start = ((), (), s32[]{:S(2)}) async-start(), calls=%async_computation.3 | async-start | bytes 6488064 | tf_op jit(solution)/shard_map/all_gather | solution.py:172
  806.6 1.5 copy-start.1
Sparse Core Ops, SparseCore 0:
  72.1 260.2 reduce-scatter.1
  335.7 93.5 all-gather.3
  432.0 90.8 all-gather.5
where the time goes:
time: 818 us; the launch traced here: 815 us
  waiting for transfers between devices  434 us (53%)
  matrix products  154 us (19%)
  other arithmetic  77 us (9%)
  local copies, waits for them, and re-layouts  53.6 us (7%)
  loops' own time  43.6 us (5%)
  blocking collectives  36.2 us (4%)
  between operations  13.5 us (2%)
    reduce_scatter x1, waiting for transfers between devices, shards(): lax.psum_scatter(jnp.einsum('wt,tai->awi', normalized_rows, slot_weight_m...  260 us
    all_gather x1, waiting for transfers between devices, shards(): key_piece = lax.all_gather(keys, 'blk', axis=0, tiled=True)  89.5 us
    all_gather x1, waiting for transfers between devices, shards(): value_piece = lax.all_gather(values, 'blk', axis=0, tiled=True)  85 us
    dot_general x32, matrix products, compute(): jnp.einsum('kgqs,skd->kgqd', weights.astype(jnp.bfloat16), value_tile_blo...  79.9 us
    dot_general x32, matrix products, compute(): jnp.einsum('qkgd,skd->kgqs', query_groups, key_block, preferred_element_t...  63.3 us
    another operation x1, loops' own time, shards(): state, unused = lax.scan(block_attention_step, state, block_data)  41.6 us
    reduce_sum x32, other arithmetic, compute(): denoms = denoms * rescale + jnp.sum(weights, -1)  34.7 us
    all_gather x1, blocking collectives, shards(): lax.all_gather(normal_vis, 'uly', axis=1, tiled=True)  23.8 us
  transfers between devices with their start and end apart: 4, of which 3 were waited for; matrix products, arithmetic and copies ran while one was open for 3% of the time, Pallas kernels for 0%

commit v1 on v0

v1 whole, which is shorter than its diff:
```python
import functools
import math

import jax
import jax.numpy as jnp
from jax import lax
from jax.experimental import pallas as pl
from jax.experimental.pallas import tpu as pltpu
from jax.sharding import PartitionSpec as P

PATCH = 64
D = 3584
HQ = 16
KVH = 4
HD = 128
GRP = 768
ROWS = 256
EXP2_SCALE = math.log2(math.e) / math.sqrt(HD)
NEG = -1e30
MESH = pl.DeviceIdType.MESH

NZ = 8
NY = 4


def from_behind(value, axis, steps):
    count = lax.axis_size(axis)
    first, last = (max(0, -steps), min(count, count - steps))
    return lax.ppermute(value, axis, [(source, source + steps) for source in range(first, last)])


def pool_frames(frames, tail_frames):
    extended = jnp.concatenate([frames, tail_frames], 0).astype(jnp.float32)
    paired_frame_sums = extended.reshape((extended.shape[0] // 2, 2) + extended.shape[1:]).sum(1)
    return (paired_frame_sums[:-1] + paired_frame_sums[1:]) * 0.25


def layer_norm(values_in, gain_vec):
    average = jnp.mean(values_in, -1, keepdims=True)
    centred = values_in - average
    variance = jnp.mean(centred * centred, -1, keepdims=True)
    return centred * lax.rsqrt(variance + 1e-06) * gain_vec


def alternate(vis_rows, text_rows, run_lengths, patch_len):
    frame_count = run_lengths.shape[0] - 1
    seq_total = vis_rows.shape[0] + text_rows.shape[0]
    run_ends = jnp.cumsum(run_lengths[:frame_count])
    starts = run_ends + patch_len * jnp.arange(frame_count, dtype=jnp.int32)
    positions = jnp.arange(seq_total, dtype=jnp.int32)[:, None]
    inside = (positions >= starts[None]) & (positions < starts[None] + patch_len)
    before = (positions >= starts[None] + patch_len).astype(jnp.int32)
    frame_ids = jnp.arange(frame_count, dtype=jnp.int32)[None]
    vis_index = jnp.sum(jnp.where(inside, frame_ids * patch_len + positions - starts[None], 0), 1)
    text_index = jnp.clip(
        positions[:, 0] - patch_len * jnp.sum(before, 1), 0, text_rows.shape[0] - 1
    )
    in_vision = jnp.any(inside, 1)
    return jnp.where(
        in_vision[:, None], jnp.take(vis_rows, vis_index, 0), jnp.take(text_rows, text_index, 0)
    )


def rotate(vectors, angles):
    half_dim = vectors.shape[-1] // 2
    cosine = jnp.cos(angles)[:, None, :]
    sine = jnp.sin(angles)[:, None, :]
    first = vectors[..., :half_dim]
    second = vectors[..., half_dim:]
    return jnp.concatenate([first * cosine - second * sine, second * cosine + first * sine], -1)


def attention_kernel(q_ref, piece_ref, out_ref, slots, top, accum, send_sem, recv_sem):
    blk = lax.axis_index("blk")
    uly = lax.axis_index("uly")
    z, place = lax.div(blk, 4), lax.rem(blk, 4)
    y_hi, core = lax.div(place, 2), lax.rem(place, 2)
    x, y_lo = lax.div(uly, 2), lax.rem(uly, 2)
    y = 2 * y_hi + y_lo

    def device(z_at, y_at, core_at):
        return (z_at * 4 + lax.div(y_at, 2) * 2 + core_at, x * 2 + lax.rem(y_at, 2))

    z_up = device(lax.rem(z + 1, NZ), y, core)
    z_down = device(lax.rem(z + NZ - 1, NZ), y, core)
    y_up = device(z, lax.rem(y + 1, NY), core)
    y_down = device(z, lax.rem(y + NY - 1, NY), core)
    sibling = device(z, y, 1 - core)

    def slot(stage, far, other):
        return stage * 8 + far * 2 + other

    def send(source, target, sem, to):
        pltpu.make_async_remote_copy(
            src_ref=slots.at[source],
            dst_ref=slots.at[target],
            send_sem=send_sem.at[sem],
            recv_sem=recv_sem.at[target],
            device_id=to,
            device_id_type=MESH,
        ).start()

    def arrived(target):
        pltpu.make_async_remote_copy(
            src_ref=slots.at[target],
            dst_ref=slots.at[target],
            send_sem=send_sem.at[target],
            recv_sem=recv_sem.at[target],
            device_id=sibling,
            device_id_type=MESH,
        ).wait_recv()

    def sent(sem):
        pltpu.make_async_remote_copy(
            src_ref=slots.at[0],
            dst_ref=slots.at[0],
            send_sem=send_sem.at[sem],
            recv_sem=recv_sem.at[0],
            device_id=sibling,
            device_id_type=MESH,
        ).wait_send()

    def spread(stage):
        mine = slot(stage, 0, 0)
        send(mine, slot(stage, 1, 0), stage * 8 + 1, y_up)
        send(mine, slot(stage, 3, 0), stage * 8 + 2, y_down)
        send(mine, slot(stage, 0, 1), stage * 8 + 4, sibling)

    def step_z(stage):
        arrived(slot(stage, 0, 0))
        odd = lax.rem(stage, 2) == 1

        @pl.when(odd & (stage + 2 < NZ))
        def _():
            send(slot(stage, 0, 0), slot(stage + 2, 0, 0), stage * 8, z_up)

        @pl.when(jnp.logical_not(odd) & (stage + 2 < NZ))
        def _():
            send(slot(stage, 0, 0), slot(stage + 2, 0, 0), stage * 8, z_down)

        spread(stage)

    def step_y(stage):
        arrived(slot(stage, 1, 0))
        arrived(slot(stage, 3, 0))
        odd = lax.rem(stage, 2) == 1

        @pl.when(odd)
        def _():
            send(slot(stage, 3, 0), slot(stage, 2, 0), stage * 8 + 3, y_down)

        @pl.when(jnp.logical_not(odd))
        def _():
            send(slot(stage, 1, 0), slot(stage, 2, 0), stage * 8 + 3, y_up)

        send(slot(stage, 1, 0), slot(stage, 1, 1), stage * 8 + 5, sibling)
        send(slot(stage, 3, 0), slot(stage, 3, 1), stage * 8 + 7, sibling)

    def step_far(stage):
        arrived(slot(stage, 2, 0))
        send(slot(stage, 2, 0), slot(stage, 2, 1), stage * 8 + 6, sibling)

    def step_sibling(stage):
        for far in range(NY):
            arrived(slot(stage, far, 1))

    barrier = pltpu.get_barrier_semaphore()
    for neighbour in (z_up, z_down, y_up, y_down, sibling):
        pl.semaphore_signal(barrier, inc=1, device_id=neighbour, device_id_type=MESH)
    pl.semaphore_wait(barrier, 5)

    slots[0] = piece_ref[...]
    send(0, slot(1, 0, 0), 0, z_up)
    send(0, slot(2, 0, 0), 64, z_down)
    spread(0)

    def unit(keys, values, first):
        ones = jnp.ones((GRP, HD), jnp.bfloat16)
        for row in range(0, GRP, ROWS):
            for head in range(2):
                at = pl.ds(head * GRP + row, ROWS)
                last = row + ROWS if first else GRP
                scores = lax.dot_general(
                    q_ref[row : row + ROWS, head * HD : (head + 1) * HD],
                    slots[keys, 0:last, :],
                    (((1,), (1,)), ((), ())),
                    preferred_element_type=jnp.float32,
                )
                if first:
                    query_at = lax.broadcasted_iota(jnp.int32, (ROWS, last), 0) + row
                    key_at = lax.broadcasted_iota(jnp.int32, (ROWS, last), 1)
                    scores = jnp.where(key_at <= query_at, scores, NEG)
                block_top = jnp.max(scores, 1, keepdims=True) * EXP2_SCALE
                if first:
                    new_top = jnp.broadcast_to(block_top, (ROWS, HD))
                else:
                    old_top = top[at, :]
                    new_top = jnp.maximum(old_top, block_top)
                weights = jnp.exp2(scores * EXP2_SCALE - new_top[:, :1]).astype(jnp.bfloat16)
                gained = jnp.dot(
                    weights,
                    jnp.concatenate([slots[values, 0:last, :], ones[0:last]], 1),
                    preferred_element_type=jnp.float32,
                )
                top[at, :] = new_top
                if first:
                    accum[at, :] = gained
                else:
                    rescale = jnp.exp2(old_top - new_top)
                    accum[at, :] = accum[at, :] * jnp.concatenate([rescale, rescale], 1) + gained

    step_y(0)
    step_z(1)
    step_z(2)
    own_pair = 1 + 2 * (1 - y_lo)
    unit(slot(0, y_lo * own_pair, 0), slot(0, (1 - y_lo) * own_pair, 0), True)
    step_far(0)
    step_y(1)

    def body(index, carry):
        stage, part = lax.div(index, 4), lax.rem(index, 4)

        @pl.when(part == 0)
        def _():
            step_sibling(stage)

            @pl.when(stage + 3 < NZ)
            def _():
                step_z(stage + 3)

        @pl.when((part == 1) & (stage + 2 < NZ))
        def _():
            step_y(stage + 2)

        @pl.when((part == 2) & (stage + 1 < NZ))
        def _():
            step_far(stage + 1)

        hops = lax.div(stage + 1, 2)
        odd = lax.rem(stage, 2)
        from_z = odd * (z - hops) + (1 - odd) * (z + hops - NZ)
        live = ((stage == 0) & (part < place)) | ((stage > 0) & (from_z >= 0))

        @pl.when(live)
        def _():
            part_hi, part_core = lax.div(part, 2), lax.rem(part, 2)
            other = lax.rem(part_core + core, 2)
            unit(
                slot(stage, lax.rem(y - 2 * part_hi + NY, NY), other),
                slot(stage, lax.rem(y - 2 * part_hi - 1 + NY, NY), other),
                False,
            )

        return carry

    lax.fori_loop(0, 4 * NZ, body, 0)

    for row in range(0, GRP, ROWS):
        for head in range(2):
            at = pl.ds(head * GRP + row, ROWS)
            out_ref[row : row + ROWS, head * HD : (head + 1) * HD] = (
                accum[at, :HD] / accum[at, HD:]
            ).astype(jnp.bfloat16)

    sent(64)

    def finish(index, carry):
        stage, kind = lax.div(index, 8), lax.rem(index, 8)

        @pl.when((kind > 0) | (stage + 2 < NZ))
        def _():
            sent(index)

        return carry

    lax.fori_loop(0, 8 * NZ, finish, 0)


def attention(queries, piece):
    return pl.pallas_call(
        attention_kernel,
        out_shape=jax.ShapeDtypeStruct((GRP, 2 * HD), jnp.bfloat16),
        in_specs=[pl.BlockSpec(memory_space=pltpu.VMEM)] * 2,
        out_specs=pl.BlockSpec(memory_space=pltpu.VMEM),
        scratch_shapes=[
            pltpu.VMEM((8 * NZ, GRP, HD), jnp.bfloat16),
            pltpu.VMEM((2 * GRP, HD), jnp.float32),
            pltpu.VMEM((2 * GRP, 2 * HD), jnp.float32),
            pltpu.SemaphoreType.DMA((8 * NZ + 1,)),
            pltpu.SemaphoreType.DMA((8 * NZ,)),
        ],
        compiler_params=pltpu.CompilerParams(
            collective_id=0, has_side_effects=True, vmem_limit_bytes=44 * 1024 * 1024
        ),
        name="gather_attention",
    )(queries, piece)


def shards(
    frames,
    vis_gain,
    proj_weight,
    text_embed,
    text_lengths,
    norm_gain,
    q_weight,
    k_weight,
    v_weight,
    q_bias,
    k_bias,
    v_bias,
):
    uly_count = lax.axis_size("uly")
    slot_index = lax.axis_index("uly")
    group_index = lax.axis_index("blk")
    halo_frames = from_behind(frames[:2], "blk", -1)
    pooled = pool_frames(frames, halo_frames)
    normal_vis = layer_norm(pooled, vis_gain).astype(jnp.bfloat16)
    vis_rows = jnp.einsum(
        "fpv,vd->fpd",
        lax.all_gather(normal_vis, "uly", axis=1, tiled=True),
        proj_weight,
        preferred_element_type=jnp.float32,
    ).astype(jnp.bfloat16)
    vis_rows = vis_rows.reshape(-1, vis_rows.shape[-1])
    sequence = alternate(vis_rows, text_embed, text_lengths[0], PATCH)
    seq_float = sequence.astype(jnp.float32)
    row_sums = lax.psum(jnp.sum(seq_float * seq_float, 1), "uly")
    normalized_rows = (seq_float * lax.rsqrt(row_sums[:, None] / D + 1e-06) * norm_gain).astype(
        jnp.bfloat16
    )
    local_rows = q_weight.shape[0]
    q_cols = 2 * HD
    slot_q = q_weight.reshape(local_rows, uly_count, q_cols)
    slot_kv = jnp.stack(
        [k_weight.reshape(local_rows, KVH, HD), v_weight.reshape(local_rows, KVH, HD)], 2
    ).reshape(local_rows, uly_count, HD)
    slot_weight_matrix = jnp.concatenate([slot_q, slot_kv], 2)
    bias_kv = jnp.stack([k_bias.reshape(KVH, HD), v_bias.reshape(KVH, HD)], 1)
    slot_bias = lax.dynamic_index_in_dim(
        jnp.concatenate([q_bias.reshape(uly_count, q_cols), bias_kv.reshape(uly_count, HD)], 1),
        slot_index,
        0,
        keepdims=False,
    )
    seq_rows = normalized_rows.shape[0]
    partials = jnp.einsum(
        "wt,tai->awi", normalized_rows, slot_weight_matrix, preferred_element_type=jnp.float32
    ).astype(jnp.bfloat16)
    received = lax.all_to_all(partials, "uly", split_axis=0, concat_axis=0, tiled=True)
    projected = jnp.sum(received.astype(jnp.float32), 0) + slot_bias
    positions = group_index * seq_rows + jnp.arange(seq_rows, dtype=jnp.int32)
    inv_freq = jnp.power(
        jnp.float32(1000000.0), -jnp.arange(HD // 2, dtype=jnp.float32) * (2.0 / HD)
    )
    angles = positions.astype(jnp.float32)[:, None] * inv_freq[None]
    queries = rotate(projected[:, :q_cols].reshape(seq_rows, 2, HD), angles).reshape(
        seq_rows, q_cols
    )
    holds_keys = slot_index % 2 == 0
    rest = projected[:, q_cols:]
    piece = jnp.where(holds_keys, rotate(rest[:, None], angles)[:, 0], rest)
    return attention(queries.astype(jnp.bfloat16), piece.astype(jnp.bfloat16))


def solution(mesh):
    placed = (
        P("blk", "uly", None),
        P(),
        P(None, "uly"),
        P("blk", "uly"),
        P("blk", None),
        P("uly"),
        P("uly", None),
        P("uly", None),
        P("uly", None),
        P(),
        P(),
        P(),
    )
    return jax.shard_map(
        shards, mesh=mesh, in_specs=placed, out_specs=P("blk", "uly"), check_vma=False
    )
```

time: 818 us -> 233 us (0.28)
  the two profiles are of different devices: /device:TPU:249 before, /device:TPU:224 now
where the time goes in v1:
time: 233 us; the launch traced here: 232 us
  Pallas kernels  88.5 us (38%)
  blocking collectives  48 us (21%)
  waiting for transfers between devices  47.7 us (20%)
  local copies, waits for them, and re-layouts  15.1 us (6%)
  other arithmetic  15.1 us (6%)
  starting transfers between devices  9.9 us (4%)
  matrix products  7.24 us (3%)
    pallas_call x1, Pallas kernels, attention(): pl.pallas_call(attention_kernel, out_shape=jax.ShapeDtypeStruct((GRP, 2 *...  88.5 us
    all_to_all x1, waiting for transfers between devices, shards(): lax.all_to_all(partials, 'uly', split_axis=0, concat_axis=0, tiled=True)  47.7 us
    all_gather x1, blocking collectives, shards(): lax.all_gather(normal_vis, 'uly', axis=1, tiled=True)  29.5 us
    psum x1, blocking collectives, shards(): row_sums = lax.psum(jnp.sum(seq_float * seq_float, 1), 'uly')  18.5 us
    dot_general x1, matrix products, shards(): jnp.einsum('wt,tai->awi', normalized_rows, slot_weight_matrix, preferred_...  6.72 us
    ppermute x1, starting transfers between devices, from_behind(): lax.ppermute(value, axis, [(source, source + steps) for source in range(f...  4.97 us
    all_to_all x1, starting transfers between devices, shards(): lax.all_to_all(partials, 'uly', split_axis=0, concat_axis=0, tiled=True)  4.93 us
  transfers between devices with their start and end apart: 2, of which 1 were waited for; matrix products, arithmetic and copies ran while one was open for 5% of the time, Pallas kernels for 0%

profile of v1, /device:TPU:224, one launch (start us, length us, event | category | flops | bytes accessed | tf_op | source)
XLA Modules:
  0.0 232.0 jit_solution(11776402178229018947)
XLA Ops:
  0.0 0.0 copy-start
  0.0 0.9 slice.32
  0.9 5.0 %collective-permute-start = (bf16[2,8,1152]{2,1,0:T(8,128)(2,1)S(1)}, bf16[2,8,1152]{2,1,0:T(8,128)(2,1)S(1)}, u32[]{:S(2)}, u32[]{:S(2)}) collective-permute-start(bf16[2,8,1152]{2,1,0:T(8,128)(2,1)S(1)} %slice.32), channel_id=1, source_target_pairs={{8,0},{16,8},{24,16},{32,24},{40,32},{48,40},{56,48},{64,56},{72,6... | collective-permute-start | bytes 110600 | tf_op jit(solution)/shard_map/ppermute | solution.py:29
  5.9 0.7 slice_bitcast_fusion.1
  6.5 0.2 reduce-window.7
  6.7 0.1 select_reduce_fusion
  6.9 0.1 fusion.26
  7.0 1.1 stack_reshape.12
  8.1 0.1 copy.28
  8.2 0.0 copy-start.6
  8.2 0.1 stack_reshape.13
  8.4 0.1 copy.29
  8.4 1.0 pad_maximum_fusion
  9.4 0.2 copy.31
  9.7 2.9 %copy.40 = bf16[56,8,8,256]{3,2,0,1:T(8,128)(2,1)} copy(bf16[56,8,8,256]{3,2,1,0:T(8,128)(2,1)} %bitcast.40) | data formatting | bytes 3670016 | tf_op jit(solution)/shard_map/reshape | solution.py:334
  12.5 2.7 %gather_fusion.1 = bf16[768,448]{1,0:T(8,128)(2,1)S(1)} fusion(bf16[512,448]{1,0:T(8,128)(2,1)S(1)} %copy.31, s32[1024]{0:T(1024)S(1)} %pad_clamp_fusion), kind=kCustom, calls=%fused_computation.1 | custom fusion | bytes 1379328 | tf_op jit(solution)/shard_map/jit(_take)/gather | solution.py:60
  15.2 0.0 collective-permute-done
  15.3 0.1 fusion.27
  15.4 0.2 multiply_reduce_fusion
  15.6 0.0 copy-done.8
  15.6 0.1 multiply_convert_fusion
  15.7 29.5 %all_gather.3 = bf16[4,64,1152]{2,1,0:T(8,128)(2,1)S(1)} all-gather(bf16[4,8,1152]{2,1,0:T(8,128)(2,1)S(1)} %multiply_convert_fusion), channel_id=1, replica_groups=mesh['blk'=32,'uly'=8] {'uly'}, dimensions={1}, use_global_device_ids=true | all-gather | bytes 663552 | tf_op jit(solution)/shard_map/all_gather | solution.py:321
  45.2 0.0 copy-done
  45.2 0.5 convolution_convert_fusion
  45.7 2.7 %gather_fusion = bf16[768,448]{1,0:T(8,128)(2,1)S(1)} fusion(bf16[256,448]{1,0:T(8,128)(2,1)S(1)} %bitcast.39, s32[1024]{0:T(1024)S(1)} %pad_clamp_fusion.1), kind=kCustom, calls=%fused_computation | custom fusion | bytes 1379328 | tf_op jit(solution)/shard_map/jit(_take)/gather | solution.py:60
  48.4 0.0 copy-start.2
  48.4 0.0 copy-start.12
  48.4 1.6 fusion.3
  50.0 18.5 %psum.7 = f32[768]{0:T(1024)S(1)} all-reduce(f32[768]{0:T(1024)S(1)} %get-tuple-element.7), channel_id=1, replica_groups=mesh['blk'=32,'uly'=8] {'uly'}, use_global_device_ids=true, to_apply=%region_8.9 | all-reduce | flops 768 | bytes 6144 | tf_op jit(solution)/shard_map/psum | solution.py:328
  68.5 0.0 copy-done.12
  68.5 6.7 %convert_bitcast_fusion = bf16[8,768,384]{1,2,0:T(8,128)(2,1)} fusion(bf16[448,8,128]{2,0,1:T(8,128)(2,1)S(1)} %bitcast.43, bf16[448,8,256]{2,0,1:T(8,128)(2,1)} %bitcast.41, bf16[768,448]{1,0:T(8,128)(2,1)} %get-tuple-element.8, f32[448]{0:T(512)S(1)} %copy-done.12, f32[768]{0:T(1024)S(1)} %add_rsqrt_fusion), kind=kOutput, calls=%fused_computation.3 | convolution fusion | flops 2123169792 | bytes 8164096 | tf_op jit(solution)/shard_map/wt,tai->awi/dot_general | solution.py:347
  75.3 4.9 %all-to-all-start = ((bf16[8,768,384]{1,2,0:T(8,128)(2,1)}), bf16[8,768,384]{1,2,0:T(8,128)(2,1)}, u32[]{:S(2)}, u32[]{:S(2)}) async-start(bf16[8,768,384]{1,2,0:T(8,128)(2,1)} %convert_bitcast_fusion), calls=%async_computation | async-start | bytes 9437184 | tf_op jit(solution)/shard_map/all_to_all | solution.py:350
  80.2 0.0 copy-done.9
  80.3 2.5 %multiply_cosine_fusion.1 = (f32[768,64]{1,0:T(8,128)}, f32[768,64]{1,0:T(8,128)}) fusion(f32[64]{0:T(128)S(1)} %multiply_power_fusion, f32[768]{0:T(1024)S(1)} %add_convert_fusion.1), kind=kLoop, calls=%fused_computation.26 | loop fusion | flops 49152 | bytes 396544 | tf_op jit(solution)/shard_map/cos | solution.py:66
  82.8 47.7 %all-to-all-done = bf16[8,768,384]{1,2,0:T(8,128)(2,1)} async-done(((bf16[8,768,384]{1,2,0:T(8,128)(2,1)}), bf16[8,768,384]{1,2,0:T(8,128)(2,1)}, u32[]{:S(2)}, u32[]{:S(2)}) %all-to-all-start) | async-done | bytes 4718624 | tf_op jit(solution)/shard_map/all_to_all | solution.py:350
  130.6 3.1 %convert_reduce_fusion = f32[768,384]{0,1:T(8,128)S(1)} fusion(bf16[8,768,384]{1,2,0:T(8,128)(2,1)} %all-to-all-done), kind=kLoop, calls=%fused_computation.2 | loop fusion | flops 4423680 | bytes 5898240 | tf_op jit(solution)/shard_map/reduce_sum | solution.py:351
  133.7 0.4 copy.33
  134.0 0.1 broadcast_add_fusion
  134.2 0.0 copy-start.1
  134.2 0.9 slice.47
  135.1 2.5 %fusion.15 = (bf16[768,1,64]{2,0,1:T(8,128)(2,1)}, bf16[768,1,64]{2,0,1:T(8,128)(2,1)}) fusion(f32[768,1,128]{2,0,1:T(8,128)S(1)} %slice_bitcast_fusion, f32[64]{0:T(128)S(1)} %multiply_power_fusion, f32[768]{0:T(1024)S(1)} %add_convert_fusion.1), kind=kLoop, calls=%fused_computation.31 | loop fusion | flops 442368 | bytes 593152 | tf_op jit(solution)/shard_map/sub | solution.py:70
  137.6 1.5 reshape.243
  139.1 2.3 subtract_convert_fusion
  141.4 1.1 pad_maximum_fusion.1
  142.5 0.1 copy.41
  142.6 0.1 fusion.18.piece_ref
  142.7 88.5 %gather_attention.1 = bf16[768,256]{1,0:T(8,128)(2,1)S(1)} custom-call(bf16[768,256]{1,0:T(8,128)(2,1)S(1)} %bitcast.38, bf16[768,128]{1,0:T(8,128)(2,1)S(1)} %fusion.18.piece_ref), custom_call_target="tpu_custom_call" | custom-call | tf_op jit(solution)/shard_map/gather_attention/pallas_call | solution.py:280
  231.2 0.7 copy.43
  (36 shorter events, 0.3 us)
Async XLA Ops:
  0.0 45.2 %copy-start = (bf16[1152,448]{0,1:T(8,128)(2,1)S(1)}, bf16[1152,448]{0,1:T(8,128)(2,1)}, u32[]{:S(2)}) copy-start(bf16[1152,448]{0,1:T(8,128)(2,1)} %param.14) | copy-start | bytes 3096580
  0.0 8.2 %copy-start.5 = (bf16[448,512]{1,0:T(8,128)(2,1)S(1)}, bf16[448,512]{1,0:T(8,128)(2,1)}, u32[]{:S(2)}) copy-start(bf16[448,512]{1,0:T(8,128)(2,1)} %param.20) | copy-start | bytes 1376260
  0.9 14.3 %collective-permute-start = (bf16[2,8,1152]{2,1,0:T(8,128)(2,1)S(1)}, bf16[2,8,1152]{2,1,0:T(8,128)(2,1)S(1)}, u32[]{:S(2)}, u32[]{:S(2)}) collective-permute-start(bf16[2,8,1152]{2,1,0:T(8,128)(2,1)S(1)} %slice.32), channel_id=1, source_target_pairs={{8,0},{16,8},{24,16},{32,24},{40,32},{48,40},{56,48},{64,56},{72,6... | collective-permute-start | bytes 110600 | tf_op jit(solution)/shard_map/ppermute | solution.py:29
  8.2 1.2 copy-start.6
  12.5 2.7 %copy-start.7 = (bf16[8,8,1152]{2,1,0:T(8,128)(2,1)S(1)}, bf16[8,8,1152]{2,1,0:T(8,128)(2,1)}, u32[]{:S(2)}) copy-start(bf16[8,8,1152]{2,1,0:T(8,128)(2,1)} %param.12) | copy-start | bytes 442372
  12.5 3.1 %copy-start.8 = (f32[1152]{0:T(1024)S(1)}, f32[1152]{0:T(1024)}, u32[]{:S(2)}) copy-start(f32[1152]{0:T(1024)} %param.13) | copy-start | bytes 13828
  48.4 20.2 %copy-start.2 = (bf16[448,4,2,128]{3,0,2,1:T(8,128)(2,1)S(1)}, bf16[448,4,2,128]{3,0,2,1:T(8,128)(2,1)}, u32[]{:S(2)}) copy-start(bf16[448,4,2,128]{3,0,2,1:T(8,128)(2,1)} %pad_maximum_fusion) | copy-start | bytes 2752516
  48.4 20.1 %copy-start.12 = (f32[448]{0:T(512)S(1)}, f32[448]{0:T(512)}, u32[]{:S(2)}) copy-start(f32[448]{0:T(512)} %param.17) | copy-start | bytes 5380
  75.3 5.0 %copy-start.9 = (f32[2048]{0:T(1024)S(1)}, f32[2048]{0:T(1024)}, u32[]{:S(2)}) copy-start(f32[2048]{0:T(1024)} %param.21) | copy-start | bytes 24580
  75.3 5.0 %copy-start.10 = (f32[512]{0:T(512)S(1)}, f32[512]{0:T(512)}, u32[]{:S(2)}) copy-start(f32[512]{0:T(512)} %param.23) | copy-start | bytes 6148
  75.3 5.0 %copy-start.11 = (f32[512]{0:T(512)S(1)}, f32[512]{0:T(512)}, u32[]{:S(2)}) copy-start(f32[512]{0:T(512)} %param.22) | copy-start | bytes 6148
  75.3 55.3 %all-to-all-start = ((bf16[8,768,384]{1,2,0:T(8,128)(2,1)}), bf16[8,768,384]{1,2,0:T(8,128)(2,1)}, u32[]{:S(2)}, u32[]{:S(2)}) async-start(bf16[8,768,384]{1,2,0:T(8,128)(2,1)} %convert_bitcast_fusion), calls=%async_computation | async-start | bytes 9437184 | tf_op jit(solution)/shard_map/all_to_all | solution.py:350
  134.2 5.0 %copy-start.1 = (f32[768,64]{1,0:T(8,128)S(1)}, f32[768,64]{1,0:T(8,128)}, u32[]{:S(2)}) copy-start(f32[768,64]{1,0:T(8,128)} %get-tuple-element.13) | copy-start | bytes 589828
  139.1 3.5 %copy-start.3 = (bf16[768,1,64]{2,0,1:T(8,128)(2,1)S(1)}, bf16[768,1,64]{2,0,1:T(8,128)(2,1)}, u32[]{:S(2)}) copy-start(bf16[768,1,64]{2,0,1:T(8,128)(2,1)} %get-tuple-element.11) | copy-start | bytes 294916
  139.1 3.5 %copy-start.4 = (bf16[768,1,64]{2,0,1:T(8,128)(2,1)S(1)}, bf16[768,1,64]{2,0,1:T(8,128)(2,1)}, u32[]{:S(2)}) copy-start(bf16[768,1,64]{2,0,1:T(8,128)(2,1)} %get-tuple-element.12) | copy-start | bytes 294916

commit v2 on v1

--- a/solution.py
+++ b/solution.py
@@ -10,8 +10,6 @@
 
 PATCH = 64
 D = 3584
-HQ = 16
-KVH = 4
 HD = 128
 GRP = 768
 ROWS = 256
@@ -21,53 +19,6 @@
 
 NZ = 8
 NY = 4
-
-
-def from_behind(value, axis, steps):
-    count = lax.axis_size(axis)
-    first, last = (max(0, -steps), min(count, count - steps))
-    return lax.ppermute(value, axis, [(source, source + steps) for source in range(first, last)])
-
-
-def pool_frames(frames, tail_frames):
-    extended = jnp.concatenate([frames, tail_frames], 0).astype(jnp.float32)
-    paired_frame_sums = extended.reshape((extended.shape[0] // 2, 2) + extended.shape[1:]).sum(1)
-    return (paired_frame_sums[:-1] + paired_frame_sums[1:]) * 0.25
-
-
-def layer_norm(values_in, gain_vec):
-    average = jnp.mean(values_in, -1, keepdims=True)
-    centred = values_in - average
-    variance = jnp.mean(centred * centred, -1, keepdims=True)
-    return centred * lax.rsqrt(variance + 1e-06) * gain_vec
-
-
-def alternate(vis_rows, text_rows, run_lengths, patch_len):
-    frame_count = run_lengths.shape[0] - 1
-    seq_total = vis_rows.shape[0] + text_rows.shape[0]
-    run_ends = jnp.cumsum(run_lengths[:frame_count])
-    starts = run_ends + patch_len * jnp.arange(frame_count, dtype=jnp.int32)
-    positions = jnp.arange(seq_total, dtype=jnp.int32)[:, None]
-    inside = (positions >= starts[None]) & (positions < starts[None] + patch_len)
-    before = (positions >= starts[None] + patch_len).astype(jnp.int32)
-    frame_ids = jnp.arange(frame_count, dtype=jnp.int32)[None]
-    vis_index = jnp.sum(jnp.where(inside, frame_ids * patch_len + positions - starts[None], 0), 1)
-    text_index = jnp.clip(
-        positions[:, 0] - patch_len * jnp.sum(before, 1), 0, text_rows.shape[0] - 1
-    )
-    in_vision = jnp.any(inside, 1)
-    return jnp.where(
-        in_vision[:, None], jnp.take(vis_rows, vis_index, 0), jnp.take(text_rows, text_index, 0)
-    )
-
-
-def rotate(vectors, angles):
-    half_dim = vectors.shape[-1] // 2
-    cosine = jnp.cos(angles)[:, None, :]
-    sine = jnp.sin(angles)[:, None, :]
-    first = vectors[..., :half_dim]
-    second = vectors[..., half_dim:]
-    return jnp.concatenate([first * cosine - second * sine, second * cosine + first * sine], -1)
 
 
 def attention_kernel(q_ref, piece_ref, out_ref, slots, top, accum, send_sem, recv_sem):
@@ -296,6 +247,313 @@
     )(queries, piece)
 
 
+TEXT_GRP = 512
+CHUNK = 128
+CHUNKS = GRP // CHUNK
+COLS = 3 * HD
+V = 1152
+
+
+def project_kernel(
+    frames_ref,
+    vis_gain_ref,
+    proj_ref,
+    text_ref,
+    lengths_ref,
+    gain_ref,
+    wq_ref,
+    wk_ref,
+    wv_ref,
+    bq_ref,
+    bk_ref,
+    bv_ref,
+    freq_ref,
+    q_ref,
+    piece_ref,
+    halo,
+    gathered,
+    rows,
+    vis,
+    text_sums,
+    vis_sums,
+    far_out,
+    far_in,
+    near_out,
+    near_in,
+    pair_out,
+    pair_in,
+    kept,
+    cosine,
+    sine,
+    done,
+    send_sem,
+    recv_sem,
+):
+    blk = lax.axis_index("blk")
+    uly = lax.axis_index("uly")
+    n_blk = lax.axis_size("blk")
+    x, y_lo = lax.div(uly, 2), lax.rem(uly, 2)
+    x_up, x_down, x_far = lax.rem(x + 1, 4), lax.rem(x + 3, 4), lax.rem(x + 2, 4)
+    up, down, pair = (blk, x_up * 2 + y_lo), (blk, x_down * 2 + y_lo), (blk, x * 2 + 1 - y_lo)
+    peers = [None] + [(blk, lax.rem(uly + step, 8)) for step in range(1, 8)]
+    earlier = (lax.rem(blk + n_blk - 1, n_blk), uly)
+    later = (lax.rem(blk + 1, n_blk), uly)
+    text_at, vis_at, gather_at, far_at, near_at, pair_at = 0, 8, 16, 24, 36, 48
+
+    def copy(source, target, sem, to):
+        return pltpu.make_async_remote_copy(
+            src_ref=source,
+            dst_ref=target,
+            send_sem=send_sem.at[sem],
+            recv_sem=recv_sem.at[sem],
+            device_id=to,
+            device_id_type=MESH,
+        )
+
+    barrier = pltpu.get_barrier_semaphore()
+    for other in peers[1:] + [earlier, later]:
+        pl.semaphore_signal(barrier, inc=1, device_id=other, device_id_type=MESH)
+    pl.semaphore_wait(barrier, 9)
+
+    halo_copy = copy(frames_ref.at[0:2], halo, 0, earlier)
+    halo_copy.start()
+    copies = [halo_copy]
+
+    def share_sums(values, sums, base):
+        squares = jnp.sum(values * values, 1, keepdims=True)
+        sums[0] = jnp.transpose(jnp.broadcast_to(squares, (values.shape[0], 128)))[0:8]
+        for step in range(1, 8):
+            sums_copy = copy(sums.at[0], sums.at[step], base + step, peers[step])
+            sums_copy.start()
+            copies.append(sums_copy)
+
+    def scales(sums, base):
+        for step in range(1, 8):
+            copy(sums.at[step], sums.at[step], base + step, peers[step]).wait_recv()
+        total = sums[0]
+        for step in range(1, 8):
+            total = total + sums[step]
+        inverse = lax.rsqrt(total[0:1] / D + 1e-06)
+        return jnp.transpose(jnp.broadcast_to(inverse, (128, inverse.shape[1])))[:, 0:1]
+
+    share_sums(text_ref[...].astype(jnp.float32), text_sums, text_at)
+
+    halo_copy.wait_recv()
+    tail = jnp.where(blk < n_blk - 1, halo[...].astype(jnp.float32), 0.0)
+    frames = frames_ref[...].astype(jnp.float32)
+    pairs = [frames[2 * i] + frames[2 * i + 1] for i in range(4)] + [tail[0] + tail[1]]
+    for i in range(4):
+        pooled = (pairs[i] + pairs[i + 1]) * 0.25
+        centred = pooled - jnp.mean(pooled, -1, keepdims=True)
+        variance = jnp.mean(centred * centred, -1, keepdims=True)
+        normal = centred * lax.rsqrt(variance + 1e-06) * vis_gain_ref[...]
+        kept[0, 8 * i : 8 * i + 8, :] = normal[:, 0:COLS]
+        kept[1, 8 * i : 8 * i + 8, :] = normal[:, COLS : 2 * COLS]
+        kept[2, 8 * i : 8 * i + 8, :] = normal[:, 2 * COLS :]
+    for i in range(3):
+        gathered[uly, :, COLS * i : COLS * i + COLS] = kept[i, 0:32, :].astype(jnp.bfloat16)
+    for step in range(1, 8):
+        gather_copy = copy(gathered.at[uly], gathered.at[uly], gather_at + step, peers[step])
+        gather_copy.start()
+        copies.append(gather_copy)
+
+    def normalize(values, scale, start):
+        rows[start : start + values.shape[0], :] = (values * scale * gain_ref[...]).astype(
+            jnp.bfloat16
+        )
+
+    normalize(text_ref[...].astype(jnp.float32), scales(text_sums, text_at), 0)
+
+    def partial(chunk, x_at, first, last):
+        left = rows[chunk * CHUNK + first : chunk * CHUNK + last, :]
+        parts = []
+        for half, other_ref in ((0, wk_ref), (1, wv_ref)):
+            q_at = pl.multiple_of(x_at * 4 * HD + half * 2 * HD, 2 * HD)
+            kv_at = pl.multiple_of(x_at * HD, HD)
+            for weight in (wq_ref[:, pl.ds(q_at, 2 * HD)], other_ref[:, pl.ds(kv_at, HD)]):
+                parts.append(jnp.dot(left, weight, preferred_element_type=jnp.float32))
+        return jnp.concatenate(parts, 1)
+
+    half = CHUNK // 2
+
+    def far_copies(chunk):
+        return (
+            copy(far_out.at[chunk, 0:half], far_in.at[chunk, 0:half], far_at + 2 * chunk, up),
+            copy(far_out.at[chunk, half:], far_in.at[chunk, half:], far_at + 2 * chunk + 1, down),
+        )
+
+    def near_copies(chunk):
+        return (
+            copy(near_out.at[chunk, 0], near_in.at[chunk, 0], near_at + 2 * chunk, up),
+            copy(near_out.at[chunk, 1], near_in.at[chunk, 1], near_at + 2 * chunk + 1, down),
+        )
+
+    def pair_copy(chunk):
+        return copy(pair_out.at[chunk], pair_in.at[chunk], pair_at + chunk, pair)
+
+    def send_far(chunk):
+        far_out[chunk] = partial(chunk, x_far, 0, CHUNK).astype(jnp.bfloat16)
+        for each in far_copies(chunk):
+            each.start()
+            copies.append(each)
+
+    def send_near(chunk):
+        for each in far_copies(chunk):
+            each.wait_recv()
+        for way, x_at, relayed in ((0, x_up, 0), (1, x_down, 1)):
+            own = partial(chunk, x_at, 0, CHUNK)
+            at = slice(relayed * half, relayed * half + half)
+            rest = slice((1 - relayed) * half, (1 - relayed) * half + half)
+            near_out[chunk, way, at, :] = (
+                own[at] + far_in[chunk, at, :].astype(jnp.float32)
+            ).astype(jnp.bfloat16)
+            near_out[chunk, way, rest, :] = own[rest].astype(jnp.bfloat16)
+        for each in near_copies(chunk):
+            each.start()
+            copies.append(each)
+
+    def send_pair(chunk):
+        for each in near_copies(chunk):
+            each.wait_recv()
+        total = (
+            partial(chunk, x, 0, CHUNK)
+            + near_in[chunk, 0].astype(jnp.float32)
+            + near_in[chunk, 1].astype(jnp.float32)
+        )
+        low, high = total[:, :COLS], total[:, COLS:]
+        mine = jnp.where(y_lo == 0, low, high)
+        pair_out[chunk] = jnp.where(y_lo == 0, high, low).astype(jnp.bfloat16)
+        kept[chunk] = mine
+        each = pair_copy(chunk)
+        each.start()
+        copies.append(each)
+
+    def run_ends():
+        ends = [lengths_ref[0, 0]]
+        for run in range(1, 4):
+            ends.append(ends[-1] + lengths_ref[0, run])
+        return ends
+
+    def text_places(index):
+        place = index
+        for end in run_ends():
+            place = place + jnp.where(index >= end, PATCH, 0)
+        return place
+
+    def vis_places(index):
+        frame = (index >> 3) & 3
+        place = (index >> 5) * 8 + (index & 7)
+        for number, end in enumerate(run_ends()):
+            place = place + jnp.where(frame == number, end + PATCH * number, 0)
+        return place
+
+    def angles(start, count, places):
+        index = lax.broadcasted_iota(jnp.int32, (count, HD), 0)
+        angle = (blk * GRP + places(index)).astype(jnp.float32) * freq_ref[...]
+        lane = lax.broadcasted_iota(jnp.int32, (count, HD), 1)
+        cosine[start : start + count, :] = jnp.cos(angle)
+        turned = jnp.sin(angle)
+        sine[start : start + count, :] = jnp.where(lane < HD // 2, -turned, turned)
+
+    def finish(chunk):
+        pair_copy(chunk).wait_recv()
+        at = slice(chunk * CHUNK, chunk * CHUNK + CHUNK)
+        total = kept[chunk] + pair_in[chunk].astype(jnp.float32)
+        kv_at = pl.multiple_of(x * HD, HD)
+        kv_bias = jnp.where(y_lo == 0, bk_ref[:, pl.ds(kv_at, HD)], bv_ref[:, pl.ds(kv_at, HD)])
+        q_bias = bq_ref[:, pl.ds(pl.multiple_of(uly * 2 * HD, 2 * HD), 2 * HD)]
+        for part, bias in enumerate((q_bias[:, :HD], q_bias[:, HD:], kv_bias)):
+            plain = total[:, part * HD : part * HD + HD] + bias
+            turned = plain * cosine[at, :] + pltpu.roll(plain, HD // 2, 1) * sine[at, :]
+            if part == 2:
+                turned = jnp.where(y_lo == 0, turned, plain)
+            done[at, part * HD : part * HD + HD] = turned.astype(jnp.bfloat16)
+
+    for chunk in range(4):
+        send_far(chunk)
+    for step in range(1, 8):
+        source = lax.rem(uly + 8 - step, 8)
+        copy(gathered.at[source], gathered.at[source], gather_at + step, peers[step]).wait_recv()
+    vis[...] = jnp.dot(
+        gathered[...].reshape(GRP - TEXT_GRP, V), proj_ref[...], preferred_element_type=jnp.float32
+    ).astype(jnp.bfloat16)
+    share_sums(vis[...].astype(jnp.float32), vis_sums, vis_at)
+    send_near(0)
+    send_near(1)
+    normalize(vis[...].astype(jnp.float32), scales(vis_sums, vis_at), TEXT_GRP)
+    send_far(4)
+    send_far(5)
+    send_near(2)
+    send_near(3)
+    angles(0, TEXT_GRP, text_places)
+    angles(TEXT_GRP, GRP - TEXT_GRP, vis_places)
+    send_near(4)
+    send_near(5)
+    for chunk in range(4):
+        send_pair(chunk)
+    for chunk in range(3):
+        finish(chunk)
+    send_pair(4)
+    finish(3)
+    send_pair(5)
+    finish(4)
+    finish(5)
+
+    index = lax.broadcasted_iota(jnp.int32, (CHUNK, TEXT_GRP), 1)
+    vis_index = lax.broadcasted_iota(jnp.int32, (CHUNK, GRP - TEXT_GRP), 1)
+    places = jnp.concatenate([text_places(index), vis_places(vis_index)], 1)
+    wanted = lax.broadcasted_iota(jnp.int32, (CHUNK, GRP), 0)
+    for chunk in range(CHUNKS):
+        at = slice(chunk * CHUNK, chunk * CHUNK + CHUNK)
+        chosen = jnp.where(places == wanted + chunk * CHUNK, 1.0, 0.0).astype(jnp.bfloat16)
+        ordered = jnp.dot(chosen, done[...], preferred_element_type=jnp.float32)
+        q_ref[at, :] = ordered[:, : 2 * HD].astype(jnp.bfloat16)
+        piece_ref[at, :] = ordered[:, 2 * HD :].astype(jnp.bfloat16)
+
+    for each in copies:
+        each.wait_send()
+
+
+def project(*operands):
+    vmem = pl.BlockSpec(memory_space=pltpu.VMEM)
+    in_specs = [vmem] * 4 + [pl.BlockSpec(memory_space=pltpu.SMEM)] + [vmem] * 8
+    bf16, f32 = jnp.bfloat16, jnp.float32
+    features = operands[3].shape[1]
+    return pl.pallas_call(
+        project_kernel,
+        out_shape=(
+            jax.ShapeDtypeStruct((GRP, 2 * HD), bf16),
+            jax.ShapeDtypeStruct((GRP, HD), bf16),
+        ),
+        in_specs=in_specs,
+        out_specs=(vmem, vmem),
+        scratch_shapes=[
+            pltpu.VMEM((2, 8, V), bf16),
+            pltpu.VMEM((8, 32, V), bf16),
+            pltpu.VMEM((GRP, features), bf16),
+            pltpu.VMEM((GRP - TEXT_GRP, features), bf16),
+            pltpu.VMEM((8, 8, TEXT_GRP), f32),
+            pltpu.VMEM((8, 8, GRP - TEXT_GRP), f32),
+            pltpu.VMEM((CHUNKS, CHUNK, 2 * COLS), bf16),
+            pltpu.VMEM((CHUNKS, CHUNK, 2 * COLS), bf16),
+            pltpu.VMEM((CHUNKS, 2, CHUNK, 2 * COLS), bf16),
+            pltpu.VMEM((CHUNKS, 2, CHUNK, 2 * COLS), bf16),
+            pltpu.VMEM((CHUNKS, CHUNK, COLS), bf16),
+            pltpu.VMEM((CHUNKS, CHUNK, COLS), bf16),
+            pltpu.VMEM((CHUNKS, CHUNK, COLS), f32),
+            pltpu.VMEM((GRP, HD), f32),
+            pltpu.VMEM((GRP, HD), f32),
+            pltpu.VMEM((GRP, COLS), bf16),
+            pltpu.SemaphoreType.DMA((54,)),
+            pltpu.SemaphoreType.DMA((54,)),
+        ],
+        compiler_params=pltpu.CompilerParams(
+            collective_id=1, has_side_effects=True, vmem_limit_bytes=44 * 1024 * 1024
+        ),
+        name="project",
+    )(*operands)
+
+
 def shards(
     frames,
     vis_gain,
@@ -310,57 +568,25 @@
     k_bias,
     v_bias,
 ):
-    uly_count = lax.axis_size("uly")
-    slot_index = lax.axis_index("uly")
-    group_index = lax.axis_index("blk")
-    halo_frames = from_behind(frames[:2], "blk", -1)
-    pooled = pool_frames(frames, halo_frames)
-    normal_vis = layer_norm(pooled, vis_gain).astype(jnp.bfloat16)
-    vis_rows = jnp.einsum(
-        "fpv,vd->fpd",
-        lax.all_gather(normal_vis, "uly", axis=1, tiled=True),
-        proj_weight,
-        preferred_element_type=jnp.float32,
-    ).astype(jnp.bfloat16)
-    vis_rows = vis_rows.reshape(-1, vis_rows.shape[-1])
-    sequence = alternate(vis_rows, text_embed, text_lengths[0], PATCH)
-    seq_float = sequence.astype(jnp.float32)
-    row_sums = lax.psum(jnp.sum(seq_float * seq_float, 1), "uly")
-    normalized_rows = (seq_float * lax.rsqrt(row_sums[:, None] / D + 1e-06) * norm_gain).astype(
-        jnp.bfloat16
-    )
-    local_rows = q_weight.shape[0]
-    q_cols = 2 * HD
-    slot_q = q_weight.reshape(local_rows, uly_count, q_cols)
-    slot_kv = jnp.stack(
-        [k_weight.reshape(local_rows, KVH, HD), v_weight.reshape(local_rows, KVH, HD)], 2
-    ).reshape(local_rows, uly_count, HD)
-    slot_weight_matrix = jnp.concatenate([slot_q, slot_kv], 2)
-    bias_kv = jnp.stack([k_bias.reshape(KVH, HD), v_bias.reshape(KVH, HD)], 1)
-    slot_bias = lax.dynamic_index_in_dim(
-        jnp.concatenate([q_bias.reshape(uly_count, q_cols), bias_kv.reshape(uly_count, HD)], 1),
-        slot_index,
-        0,
-        keepdims=False,
-    )
-    seq_rows = normalized_rows.shape[0]
-    partials = jnp.einsum(
-        "wt,tai->awi", normalized_rows, slot_weight_matrix, preferred_element_type=jnp.float32
-    ).astype(jnp.bfloat16)
-    received = lax.all_to_all(partials, "uly", split_axis=0, concat_axis=0, tiled=True)
-    projected = jnp.sum(received.astype(jnp.float32), 0) + slot_bias
-    positions = group_index * seq_rows + jnp.arange(seq_rows, dtype=jnp.int32)
     inv_freq = jnp.power(
         jnp.float32(1000000.0), -jnp.arange(HD // 2, dtype=jnp.float32) * (2.0 / HD)
     )
-    angles = positions.astype(jnp.float32)[:, None] * inv_freq[None]
-    queries = rotate(projected[:, :q_cols].reshape(seq_rows, 2, HD), angles).reshape(
-        seq_rows, q_cols
+    queries, piece = project(
+        frames,
+        vis_gain[None],
+        proj_weight,
+        text_embed,
+        text_lengths,
+        norm_gain[None],
+        q_weight,
+        k_weight,
+        v_weight,
+        q_bias[None],
+        k_bias[None],
+        v_bias[None],
+        jnp.concatenate([inv_freq, inv_freq])[None],
     )
-    holds_keys = slot_index % 2 == 0
-    rest = projected[:, q_cols:]
-    piece = jnp.where(holds_keys, rotate(rest[:, None], angles)[:, 0], rest)
-    return attention(queries.astype(jnp.bfloat16), piece.astype(jnp.bfloat16))
+    return attention(queries, piece)
 
 
 def solution(mesh):

time: 233 us -> 164 us (0.70)
  Pallas kernels: 88.5 us -> 152 us
  blocking collectives: 48 us -> 0 us
  waiting for transfers between devices: 47.7 us -> 0 us
  other arithmetic: 15.1 us -> 0.6 us
  starting transfers between devices: 9.9 us -> 0 us
  matrix products: 7.24 us -> 0 us
  local copies, waits for them, and re-layouts: 15.1 us -> 10.7 us
    pallas_call x0 -> x1, Pallas kernels: none -> 60 us  [project(): pl.pallas_call(project_kernel, out_shape=(jax.ShapeDtypeStruct((GRP, 2 *...]
    all_to_all x1 -> x0, waiting for transfers between devices: 47.7 us -> none  [shards(): lax.all_to_all(partials, 'uly', split_axis=0, concat_axis=0, tiled=True)]
    all_gather x1 -> x0, blocking collectives: 29.5 us -> none  [shards(): lax.all_gather(normal_vis, 'uly', axis=1, tiled=True)]
    psum x1 -> x0, blocking collectives: 18.5 us -> none  [shards(): row_sums = lax.psum(jnp.sum(seq_float * seq_float, 1), 'uly')]
    unnamed x29 -> x23, local copies, waits for them, and re-layouts: 1.07 us -> 10 us
    dot_general x2 -> x0, matrix products: 7.24 us -> none  [the longest x1 6.72 us: shards(): jnp.einsum('wt,tai->awi', normalized_rows, slot_weight_matrix, preferred_...]
    gather x2 -> x0, local copies, waits for them, and re-layouts: 5.36 us -> none  [the longest x1 2.68 us: alternate(): jnp.take(vis_rows, vis_index, 0)]
    reduce_sum x6 -> x0, other arithmetic: 5.07 us -> none  [the longest x1 3.09 us: shards(): projected = jnp.sum(received.astype(jnp.float32), 0) + slot_bias]
  transfers between devices with their start and end apart: 2 -> 0, of which waited for: 1 -> 0; matrix products, arithmetic and copies ran while one was open for 5% -> 0% of each run, Pallas kernels for 0% -> 0%
where the time goes in v2:
time: 164 us; the launch traced here: 163 us
  Pallas kernels  152 us (93%)
  local copies, waits for them, and re-layouts  10.7 us (7%)
    pallas_call x1, Pallas kernels, attention(): pl.pallas_call(attention_kernel, out_shape=jax.ShapeDtypeStruct((GRP, 2 *...  92 us
    pallas_call x1, Pallas kernels, project(): pl.pallas_call(project_kernel, out_shape=(jax.ShapeDtypeStruct((GRP, 2 *...  60 us
    unnamed x23, local copies, waits for them, and re-layouts  10 us

profile of v2, /device:TPU:224, one launch (start us, length us, event | category | flops | bytes accessed | tf_op | source)
XLA Modules:
  0.0 163.4 jit_solution(7465879404319545968)
XLA Ops:
  0.0 0.0 copy-start.4
  0.0 0.0 copy-start
  0.0 0.6 maximum_bitcast_fusion.freq_ref
  0.6 0.7 broadcast_in_dim.18.vis_gain_ref
  1.3 1.2 copy.14.text_ref
  2.5 1.7 %copy.13.proj_ref = bf16[1152,448]{1,0:T(8,128)(2,1)S(1)} copy(bf16[1152,448]{0,1:T(8,128)(2,1)} %param.14) | data formatting | bytes 2064384 | tf_op args[2]
  4.3 0.0 copy-done.4
  4.3 0.0 copy-done
  4.3 0.0 copy-start.1
  4.3 1.0 copy-done.1
  5.3 0.0 copy-start.2
  5.3 1.0 copy-done.2
  6.4 0.0 copy-start.3
  6.4 0.9 copy-done.3
  7.3 0.0 copy-start.5
  7.3 0.7 copy-done.5
  7.9 0.0 copy-start.6
  7.9 0.7 copy-done.6
  8.6 0.0 copy-start.7
  8.6 0.7 copy-done.7
  9.3 0.0 copy-start.8
  9.3 0.7 copy-done.8
  10.0 0.0 copy-start.9
  10.0 0.7 copy-done.9
  10.6 60.0 %project.1 = (bf16[768,256]{1,0:T(8,128)(2,1)S(1)}, bf16[768,128]{1,0:T(8,128)(2,1)S(1)}) custom-call(bf16[8,8,1152]{2,1,0:T(8,128)(2,1)S(1)} %copy-done.3, f32[1,1152]{1,0:T(1,128)S(1)} %broadcast_in_dim.18.vis_gain_ref, bf16[1152,448]{1,0:T(8,128)(2,1)S(1)} %copy.13.proj_ref, bf16[512,448]{1,0:T(8,128)(2,1)S(1)} %copy.14.text_ref, s32[1,5]{1,0:T(1,128)S(1)} %copy-done.8, ...), custom_call_target="tpu_custom_call" | custom-call | tf_op jit(solution)/shard_map/project/pallas_call | solution.py:522
  70.7 92.0 %gather_attention.1 = bf16[768,256]{1,0:T(8,128)(2,1)S(1)} custom-call(bf16[768,256]{1,0:T(8,128)(2,1)S(1)} %get-tuple-element.7.q_ref, bf16[768,128]{1,0:T(8,128)(2,1)S(1)} %get-tuple-element.8.piece_ref), custom_call_target="tpu_custom_call" | custom-call | tf_op jit(solution)/shard_map/gather_attention/pallas_call | solution.py:231
  162.7 0.7 copy.16
  (1 shorter events, 0.0 us)
Async XLA Ops:
  0.0 4.3 %copy-start.4 = (f32[2048]{0:T(1024)S(1)}, f32[2048]{0:T(1024)}, u32[]{:S(2)}) copy-start(f32[2048]{0:T(1024)} %param.21) | copy-start | bytes 24580
  0.0 4.3 %copy-start = (bf16[448,2048]{1,0:T(8,128)(2,1)S(1)}, bf16[448,2048]{1,0:T(8,128)(2,1)}, u32[]{:S(2)}) copy-start(bf16[448,2048]{1,0:T(8,128)(2,1)} %wq_ref.1) | copy-start | bytes 5505028
  4.3 1.0 copy-start.1
  5.3 1.0 copy-start.2
  6.4 0.9 copy-start.3
  7.3 0.7 copy-start.5
  7.9 0.7 copy-start.6
  8.6 0.7 copy-start.7
  9.3 0.7 copy-start.8
  10.0 0.7 copy-start.9

commit v3 on v1

v3 whole, which is shorter than its diff:
```python
import math

import jax
import jax.numpy as jnp
import numpy as np
from jax import lax
from jax.experimental import pallas as pl
from jax.experimental.pallas import tpu as pltpu
from jax.sharding import PartitionSpec as P

PATCH = 64
D = 3584
V = 1152
HD = 128
GRP = 768
TEXT_GRP = 512
VIS_GRP = 256
CHUNK = 128
CHUNKS = GRP // CHUNK
ROWS = 256
EXP2_SCALE = math.log2(math.e) / math.sqrt(HD)
NEG = -1e30
MESH = pl.DeviceIdType.MESH

NZ = 8
NY = 4

KV, Q = 0, 1
WIDTH = (2 * HD, 4 * HD)

AT_HALO, AT_TEXT, AT_VIS, AT_GATHER = 0, 0, 8, 16
AT_FAR, AT_NEAR, AT_PAIR = (24, 36), (48, 60), (72, 78)
AT_SLOTS = 84


def kernel(
    frames_hbm,
    vis_gain_hbm,
    proj_hbm,
    text_hbm,
    lengths_hbm,
    gain_hbm,
    wq_hbm,
    wk_hbm,
    wv_hbm,
    bq_hbm,
    bk_hbm,
    bv_hbm,
    freq_hbm,
    out_ref,
    frames_ref,
    vis_gain_ref,
    proj_ref,
    text_ref,
    lengths_ref,
    gain_ref,
    wq_ref,
    wk_ref,
    wv_ref,
    bq_ref,
    bk_ref,
    bv_ref,
    freq_ref,
    halo,
    normal_rows,
    gathered,
    rows,
    vis,
    text_sums,
    vis_sums,
    far_out_kv,
    far_in_kv,
    near_out_kv,
    near_in_kv,
    pair_out_kv,
    pair_in_kv,
    kept_kv,
    far_out_q,
    far_in_q,
    near_out_q,
    near_in_q,
    pair_out_q,
    pair_in_q,
    kept_q,
    cosine,
    sine,
    done_kv,
    done_q,
    queries,
    slots,
    top,
    accum,
    load_sem,
    send_sem,
    recv_sem,
):
    blk = lax.axis_index("blk")
    uly = lax.axis_index("uly")
    n_blk = lax.axis_size("blk")
    z, place = lax.div(blk, 4), lax.rem(blk, 4)
    y_hi, core = lax.div(place, 2), lax.rem(place, 2)
    x, y_lo = lax.div(uly, 2), lax.rem(uly, 2)
    y = 2 * y_hi + y_lo

    loads = [
        pltpu.make_async_copy(source, target, load_sem.at[number])
        for number, (source, target) in enumerate(
            (
                (frames_hbm, frames_ref),
                (text_hbm, text_ref),
                (vis_gain_hbm, vis_gain_ref),
                (gain_hbm, gain_ref),
                (wk_hbm, wk_ref),
                (wv_hbm, wv_ref),
                (proj_hbm, proj_ref),
                (lengths_hbm, lengths_ref),
                (freq_hbm, freq_ref),
                (bk_hbm, bk_ref),
                (bv_hbm, bv_ref),
                (bq_hbm, bq_ref),
                (wq_hbm, wq_ref),
            )
        )
    ]
    for load in loads:
        load.start()

    def device(z_at, y_at, core_at):
        return (z_at * 4 + lax.div(y_at, 2) * 2 + core_at, x * 2 + lax.rem(y_at, 2))

    z_up = device(lax.rem(z + 1, NZ), y, core)
    z_down = device(lax.rem(z + NZ - 1, NZ), y, core)
    y_up = device(z, lax.rem(y + 1, NY), core)
    y_down = device(z, lax.rem(y + NY - 1, NY), core)
    sibling = device(z, y, 1 - core)
    x_up, x_down, x_far = lax.rem(x + 1, 4), lax.rem(x + 3, 4), lax.rem(x + 2, 4)
    up, down, pair = (blk, x_up * 2 + y_lo), (blk, x_down * 2 + y_lo), (blk, x * 2 + 1 - y_lo)
    peers = [None] + [(blk, lax.rem(uly + step, 8)) for step in range(1, 8)]
    earlier = (lax.rem(blk + n_blk - 1, n_blk), uly)
    later = (lax.rem(blk + 1, n_blk), uly)

    barrier = pltpu.get_barrier_semaphore()
    others = peers[1:] + [earlier, later, z_up, z_down, y_up, y_down, sibling]
    for other in others:
        pl.semaphore_signal(barrier, inc=1, device_id=other, device_id_type=MESH)
    pl.semaphore_wait(barrier, len(others))

    copies = []

    def copy(source, target, sem, to):
        return pltpu.make_async_remote_copy(
            src_ref=source,
            dst_ref=target,
            send_sem=send_sem.at[sem],
            recv_sem=recv_sem.at[sem],
            device_id=to,
            device_id_type=MESH,
        )

    def start(each):
        each.start()
        copies.append(each)

    loads[0].wait()
    halo_copy = copy(frames_ref.at[0:2], halo, AT_HALO, earlier)
    start(halo_copy)

    def send_sums(sums, base):
        for step in range(1, 8):
            start(copy(sums.at[0], sums.at[step], base + step, peers[step]))

    def scales(sums, base):
        for step in range(1, 8):
            copy(sums.at[step], sums.at[step], base + step, peers[step]).wait_recv()
        total = sums[0]
        for step in range(1, 8):
            total = total + sums[step]
        return lax.rsqrt(total[0:1] / D + 1e-06)

    loads[1].wait()
    text = text_ref[...].astype(jnp.float32)
    text_sums[0] = jnp.broadcast_to(jnp.sum(text * text, 0, keepdims=True), (8, TEXT_GRP))
    send_sums(text_sums, AT_TEXT)

    for load in loads[2:6]:
        load.wait()
    halo_copy.wait_recv()
    tail = jnp.where(blk < n_blk - 1, halo[...].astype(jnp.float32), 0.0)
    frames = frames_ref[...].astype(jnp.float32)
    pairs = [frames[2 * i] + frames[2 * i + 1] for i in range(4)] + [tail[0] + tail[1]]
    for i in range(4):
        pooled = (pairs[i] + pairs[i + 1]) * 0.25
        centred = pooled - jnp.mean(pooled, -1, keepdims=True)
        variance = jnp.mean(centred * centred, -1, keepdims=True)
        normal_rows[8 * i : 8 * i + 8, :] = (
            centred * lax.rsqrt(variance + 1e-06) * vis_gain_ref[...]
        )
    gathered[uly] = normal_rows[...].astype(jnp.bfloat16)
    for step in range(1, 8):
        start(copy(gathered.at[uly], gathered.at[uly], AT_GATHER + step, peers[step]))

    scaled_text = jnp.transpose(text_ref[...].astype(jnp.float32) * scales(text_sums, AT_TEXT))
    rows[0:TEXT_GRP, :] = (scaled_text * gain_ref[...]).astype(jnp.bfloat16)

    far_out, far_in = (far_out_kv, far_out_q), (far_in_kv, far_in_q)
    near_out, near_in = (near_out_kv, near_out_q), (near_in_kv, near_in_q)
    pair_out, pair_in = (pair_out_kv, pair_out_q), (pair_in_kv, pair_in_q)
    kept, done = (kept_kv, kept_q), (done_kv, done_q)
    half = CHUNK // 2

    def partial(kind, chunk, x_at):
        left = rows[chunk * CHUNK : (chunk + 1) * CHUNK, :]
        if kind == Q:
            weight = wq_ref[:, pl.ds(pl.multiple_of(x_at * 4 * HD, 4 * HD), 4 * HD)]
            return jnp.dot(left, weight, preferred_element_type=jnp.float32)
        at = pl.ds(pl.multiple_of(x_at * HD, HD), HD)
        return jnp.concatenate(
            [
                jnp.dot(left, weight[:, at], preferred_element_type=jnp.float32)
                for weight in (wk_ref, wv_ref)
            ],
            1,
        )

    def far_copies(kind, chunk):
        out, into, base = far_out[kind].at[chunk], far_in[kind].at[chunk], AT_FAR[kind] + 2 * chunk
        return (
            copy(out.at[0:half], into.at[0:half], base, up),
            copy(out.at[half:CHUNK], into.at[half:CHUNK], base + 1, down),
        )

    def near_copies(kind, chunk):
        out, into = near_out[kind].at[chunk], near_in[kind].at[chunk]
        base = AT_NEAR[kind] + 2 * chunk
        return (
            copy(out.at[0], into.at[0], base, up),
            copy(out.at[1], into.at[1], base + 1, down),
        )

    def pair_copy(kind, chunk):
        return copy(
            pair_out[kind].at[chunk], pair_in[kind].at[chunk], AT_PAIR[kind] + chunk, pair
        )

    def send_far(kind, chunk):
        far_out[kind][chunk] = partial(kind, chunk, x_far).astype(jnp.bfloat16)
        for each in far_copies(kind, chunk):
            start(each)

    def send_near(kind, chunk):
        for each in far_copies(kind, chunk):
            each.wait_recv()
        for way, x_at in ((0, x_up), (1, x_down)):
            own = partial(kind, chunk, x_at)
            relayed = slice(way * half, way * half + half)
            rest = slice((1 - way) * half, (1 - way) * half + half)
            near_out[kind][chunk, way, relayed, :] = (
                own[relayed] + far_in[kind][chunk, relayed, :].astype(jnp.float32)
            ).astype(jnp.bfloat16)
            near_out[kind][chunk, way, rest, :] = own[rest].astype(jnp.bfloat16)
        for each in near_copies(kind, chunk):
            start(each)

    def send_pair(kind, chunk):
        for each in near_copies(kind, chunk):
            each.wait_recv()
        total = (
            partial(kind, chunk, x)
            + near_in[kind][chunk, 0].astype(jnp.float32)
            + near_in[kind][chunk, 1].astype(jnp.float32)
        )
        middle = WIDTH[kind] // 2
        low, high = total[:, :middle], total[:, middle:]
        kept[kind][chunk] = jnp.where(y_lo == 0, low, high)
        pair_out[kind][chunk] = jnp.where(y_lo == 0, high, low).astype(jnp.bfloat16)
        start(pair_copy(kind, chunk))

    def finish(kind, chunk):
        pair_copy(kind, chunk).wait_recv()
        at = slice(chunk * CHUNK, chunk * CHUNK + CHUNK)
        total = kept[kind][chunk] + pair_in[kind][chunk].astype(jnp.float32)
        if kind == KV:
            bias_at = pl.ds(pl.multiple_of(x * HD, HD), HD)
            total = total + jnp.where(y_lo == 0, bk_ref[:, bias_at], bv_ref[:, bias_at])
        else:
            total = total + bq_ref[:, pl.ds(pl.multiple_of(uly * 2 * HD, 2 * HD), 2 * HD)]
        for head in range(WIDTH[kind] // (2 * HD)):
            columns = slice(head * HD, head * HD + HD)
            plain = total[:, columns]
            turned = plain * cosine[at, :] + pltpu.roll(plain, HD // 2, 1) * sine[at, :]
            if kind == KV:
                turned = jnp.where(y_lo == 0, turned, plain)
            done[kind][at, columns] = turned.astype(jnp.bfloat16)

    def run_ends():
        ends = [lengths_ref[0, 0]]
        for run in range(1, 4):
            ends.append(ends[-1] + lengths_ref[0, run])
        return ends

    def text_places(index):
        place_of = index
        for end in run_ends():
            place_of = place_of + jnp.where(index >= end, PATCH, 0)
        return place_of

    def vis_places(index):
        frame = (index >> 3) & 3
        place_of = (index >> 5) * 8 + (index & 7)
        for number, end in enumerate(run_ends()):
            place_of = place_of + jnp.where(frame == number, end + PATCH * number, 0)
        return place_of

    def angles(first, count, places):
        index = lax.broadcasted_iota(jnp.int32, (count, HD), 0)
        angle = (blk * GRP + places(index)).astype(jnp.float32) * freq_ref[...]
        lane = lax.broadcasted_iota(jnp.int32, (count, HD), 1)
        cosine[first : first + count, :] = jnp.cos(angle)
        turned = jnp.sin(angle)
        sine[first : first + count, :] = jnp.where(lane < HD // 2, -turned, turned)

    def ordered(kind, write):
        index = lax.broadcasted_iota(jnp.int32, (CHUNK, TEXT_GRP), 1)
        vis_index = lax.broadcasted_iota(jnp.int32, (CHUNK, VIS_GRP), 1)
        places = jnp.concatenate([text_places(index), vis_places(vis_index)], 1)
        wanted = lax.broadcasted_iota(jnp.int32, (CHUNK, GRP), 0)
        for chunk in range(CHUNKS):
            chosen = jnp.where(places == wanted + chunk * CHUNK, 1.0, 0.0).astype(jnp.bfloat16)
            result = jnp.dot(chosen, done[kind][...], preferred_element_type=jnp.float32)
            write(slice(chunk * CHUNK, chunk * CHUNK + CHUNK), result.astype(jnp.bfloat16))

    def slot(stage, far, other):
        return stage * 8 + far * 2 + other

    def slot_copy(source, target, sem, to):
        return pltpu.make_async_remote_copy(
            src_ref=slots.at[source],
            dst_ref=slots.at[target],
            send_sem=send_sem.at[AT_SLOTS + sem],
            recv_sem=recv_sem.at[AT_SLOTS + target],
            device_id=to,
            device_id_type=MESH,
        )

    def send(source, target, sem, to):
        slot_copy(source, target, sem, to).start()

    def arrived(target):
        slot_copy(target, target, target, sibling).wait_recv()

    def spread(stage):
        mine = slot(stage, 0, 0)
        send(mine, slot(stage, 1, 0), stage * 8 + 1, y_up)
        send(mine, slot(stage, 3, 0), stage * 8 + 2, y_down)
        send(mine, slot(stage, 0, 1), stage * 8 + 4, sibling)

    def step_z(stage):
        arrived(slot(stage, 0, 0))
        odd = lax.rem(stage, 2) == 1

        @pl.when(odd & (stage + 2 < NZ))
        def _():
            send(slot(stage, 0, 0), slot(stage + 2, 0, 0), stage * 8, z_up)

        @pl.when(jnp.logical_not(odd) & (stage + 2 < NZ))
        def _():
            send(slot(stage, 0, 0), slot(stage + 2, 0, 0), stage * 8, z_down)

        spread(stage)

    def step_y(stage):
        arrived(slot(stage, 1, 0))
        arrived(slot(stage, 3, 0))
        odd = lax.rem(stage, 2) == 1

        @pl.when(odd)
        def _():
            send(slot(stage, 3, 0), slot(stage, 2, 0), stage * 8 + 3, y_down)

        @pl.when(jnp.logical_not(odd))
        def _():
            send(slot(stage, 1, 0), slot(stage, 2, 0), stage * 8 + 3, y_up)

        send(slot(stage, 1, 0), slot(stage, 1, 1), stage * 8 + 5, sibling)
        send(slot(stage, 3, 0), slot(stage, 3, 1), stage * 8 + 7, sibling)

    def step_far(stage):
        arrived(slot(stage, 2, 0))
        send(slot(stage, 2, 0), slot(stage, 2, 1), stage * 8 + 6, sibling)

    def step_sibling(stage):
        for far in range(NY):
            arrived(slot(stage, far, 1))

    def scores_of(keys, count, row, head, last):
        block = slots[pl.ds(keys, count), 0:last, :].reshape(count * last, HD)
        return lax.dot_general(
            queries[row : row + ROWS, head * HD : (head + 1) * HD],
            block,
            (((1,), (1,)), ((), ())),
            preferred_element_type=jnp.float32,
        )

    def absorb(values, count, row, head, last, scores, first):
        at = pl.ds(head * GRP + row, ROWS)
        if first:
            query_at = lax.broadcasted_iota(jnp.int32, (ROWS, last), 0) + row
            key_at = lax.broadcasted_iota(jnp.int32, (ROWS, last), 1)
            scores = jnp.where(key_at <= query_at, scores, NEG)
        block_top = jnp.max(scores, 1, keepdims=True) * EXP2_SCALE
        if first:
            new_top = jnp.broadcast_to(block_top, (ROWS, HD))
        else:
            old_top = top[at, :]
            new_top = jnp.maximum(old_top, block_top)
        weights = jnp.exp2(scores * EXP2_SCALE - new_top[:, :1]).astype(jnp.bfloat16)
        block = slots[pl.ds(values, count), 0:last, :].reshape(count * last, HD)
        gained = jnp.dot(
            weights,
            jnp.concatenate([block, jnp.ones(block.shape, jnp.bfloat16)], 1),
            preferred_element_type=jnp.float32,
        )
        top[at, :] = new_top
        if first:
            accum[at, :] = gained
        else:
            rescale = jnp.exp2(old_top - new_top)
            accum[at, :] = accum[at, :] * jnp.concatenate([rescale, rescale], 1) + gained

    def unit(keys, values, count, first):
        waiting = None
        for row in range(0, GRP, ROWS):
            for head in range(2):
                last = row + ROWS if first else GRP
                scores = scores_of(keys, count, row, head, last)
                if waiting is not None:
                    absorb(values, count, *waiting, first)
                waiting = (row, head, last, scores)
        absorb(values, count, *waiting, first)

    for chunk in range(4):
        send_far(KV, chunk)
    loads[6].wait()
    for step in range(1, 8):
        source = lax.rem(uly + 8 - step, 8)
        copy(gathered.at[source], gathered.at[source], AT_GATHER + step, peers[step]).wait_recv()
    vis[...] = lax.dot_general(
        gathered[...].reshape(VIS_GRP, V),
        proj_ref[...],
        (((1,), (1,)), ((), ())),
        preferred_element_type=jnp.float32,
    ).astype(jnp.bfloat16)
    vis_float = vis[...].astype(jnp.float32)
    squares = jnp.sum(vis_float * vis_float, 1, keepdims=True)
    vis_sums[0] = jnp.transpose(jnp.broadcast_to(squares, (VIS_GRP, 128)))[0:8]
    send_sums(vis_sums, AT_VIS)
    for chunk in range(4):
        send_near(KV, chunk)
    inverse = jnp.transpose(jnp.broadcast_to(scales(vis_sums, AT_VIS), (128, VIS_GRP)))[:, 0:1]
    rows[TEXT_GRP:GRP, :] = (vis[...].astype(jnp.float32) * inverse * gain_ref[...]).astype(
        jnp.bfloat16
    )
    send_far(KV, 4)
    send_far(KV, 5)
    for load in loads[7:]:
        load.wait()
    for chunk in range(4):
        send_far(Q, chunk)
    angles(0, TEXT_GRP, text_places)
    send_near(KV, 4)
    send_near(KV, 5)
    for chunk in range(4):
        send_pair(KV, chunk)
    angles(TEXT_GRP, VIS_GRP, vis_places)
    for chunk in range(4):
        finish(KV, chunk)
    send_pair(KV, 4)
    send_pair(KV, 5)
    finish(KV, 4)
    finish(KV, 5)

    def write_piece(at, result):
        slots[0, at, :] = result

    ordered(KV, write_piece)
    send(0, slot(1, 0, 0), 0, z_up)
    send(0, slot(2, 0, 0), 64, z_down)
    spread(0)

    send_far(Q, 4)
    send_far(Q, 5)
    for chunk in range(3):
        send_near(Q, chunk)
    step_y(0)
    step_z(1)
    step_z(2)
    for chunk in range(3, 6):
        send_near(Q, chunk)
    step_far(0)
    step_y(1)
    for chunk in range(3):
        send_pair(Q, chunk)
    step_z(3)
    step_y(2)
    step_far(1)
    for chunk in range(3):
        finish(Q, chunk)
    for chunk in range(3, 6):
        send_pair(Q, chunk)
    step_z(4)
    step_y(3)
    step_far(2)
    for chunk in range(3, 6):
        finish(Q, chunk)

    def write_queries(at, result):
        queries[at, :] = result

    ordered(Q, write_queries)
    step_z(5)

    own_pair = 1 + 2 * (1 - y_lo)
    unit(slot(0, y_lo * own_pair, 0), slot(0, (1 - y_lo) * own_pair, 0), 1, True)
    step_sibling(0)

    def stage_zero(part, carry):
        @pl.when(part < place)
        def _():
            part_hi, part_core = lax.div(part, 2), lax.rem(part, 2)
            other = lax.rem(part_core + core, 2)
            unit(
                slot(0, lax.rem(y - 2 * part_hi + NY, NY), other),
                slot(0, lax.rem(y - 2 * part_hi - 1 + NY, NY), other),
                1,
                False,
            )

        return carry

    lax.fori_loop(0, 3, stage_zero, 0)

    def later_stages(index, carry):
        stage, part_hi = lax.div(index, 2), lax.rem(index, 2)

        @pl.when(part_hi == 0)
        def _():
            @pl.when(stage + 5 < NZ)
            def _():
                step_z(stage + 5)

            @pl.when(stage + 3 < NZ)
            def _():
                step_y(stage + 3)

            @pl.when(stage + 2 < NZ)
            def _():
                step_far(stage + 2)

            step_sibling(stage)

        hops = lax.div(stage + 1, 2)
        odd = lax.rem(stage, 2)
        from_z = odd * (z - hops) + (1 - odd) * (z + hops - NZ)

        @pl.when(from_z >= 0)
        def _():
            unit(
                slot(stage, lax.rem(y - 2 * part_hi + NY, NY), 0),
                slot(stage, lax.rem(y - 2 * part_hi - 1 + NY, NY), 0),
                2,
                False,
            )

        return carry

    lax.fori_loop(2, 2 * NZ, later_stages, 0)

    for row in range(0, GRP, ROWS):
        for head in range(2):
            at = pl.ds(head * GRP + row, ROWS)
            out_ref[row : row + ROWS, head * HD : (head + 1) * HD] = (
                accum[at, :HD] / accum[at, HD:]
            ).astype(jnp.bfloat16)

    for each in copies:
        each.wait_send()
    slot_copy(0, 0, 64, sibling).wait_send()

    def settle(index, carry):
        stage, kind = lax.div(index, 8), lax.rem(index, 8)

        @pl.when((kind > 0) | (stage + 2 < NZ))
        def _():
            slot_copy(0, 0, index, sibling).wait_send()

        return carry

    lax.fori_loop(0, 8 * NZ, settle, 0)


def shards(
    frames,
    vis_gain,
    proj_weight,
    text_embed,
    text_lengths,
    norm_gain,
    q_weight,
    k_weight,
    v_weight,
    q_bias,
    k_bias,
    v_bias,
):
    bf16, f32 = jnp.bfloat16, jnp.float32
    inv_freq = np.power(1e6, -np.arange(HD // 2) * (2.0 / HD)).astype(np.float32)
    operands = (
        frames,
        vis_gain[None],
        proj_weight.T,
        text_embed.T,
        text_lengths,
        norm_gain[None],
        q_weight,
        k_weight,
        v_weight,
        q_bias[None],
        k_bias[None],
        v_bias[None],
        jnp.asarray(np.concatenate([inv_freq, inv_freq])[None]),
    )
    landing = [pltpu.VMEM(operand.shape, operand.dtype) for operand in operands]
    landing[4] = pltpu.SMEM(text_lengths.shape, text_lengths.dtype)
    features = text_embed.shape[1]
    sums = []
    for width in WIDTH:
        sums += [
            pltpu.VMEM((CHUNKS, CHUNK, width), bf16),
            pltpu.VMEM((CHUNKS, CHUNK, width), bf16),
            pltpu.VMEM((CHUNKS, 2, CHUNK, width), bf16),
            pltpu.VMEM((CHUNKS, 2, CHUNK, width), bf16),
            pltpu.VMEM((CHUNKS, CHUNK, width // 2), bf16),
            pltpu.VMEM((CHUNKS, CHUNK, width // 2), bf16),
            pltpu.VMEM((CHUNKS, CHUNK, width // 2), f32),
        ]
    return pl.pallas_call(
        kernel,
        out_shape=jax.ShapeDtypeStruct((GRP, 2 * HD), bf16),
        in_specs=[pl.BlockSpec(memory_space=pltpu.HBM)] * len(operands),
        out_specs=pl.BlockSpec(memory_space=pltpu.VMEM),
        scratch_shapes=landing
        + [
            pltpu.VMEM((2, 8, V), bf16),
            pltpu.VMEM((32, V), f32),
            pltpu.VMEM((8, 32, V), bf16),
            pltpu.VMEM((GRP, features), bf16),
            pltpu.VMEM((VIS_GRP, features), bf16),
            pltpu.VMEM((8, 8, TEXT_GRP), f32),
            pltpu.VMEM((8, 8, VIS_GRP), f32),
        ]
        + sums
        + [
            pltpu.VMEM((GRP, HD), f32),
            pltpu.VMEM((GRP, HD), f32),
            pltpu.VMEM((GRP, HD), bf16),
            pltpu.VMEM((GRP, 2 * HD), bf16),
            pltpu.VMEM((GRP, 2 * HD), bf16),
            pltpu.VMEM((8 * NZ, GRP, HD), bf16),
            pltpu.VMEM((2 * GRP, HD), f32),
            pltpu.VMEM((2 * GRP, 2 * HD), f32),
            pltpu.SemaphoreType.DMA((len(operands),)),
            pltpu.SemaphoreType.DMA((AT_SLOTS + 8 * NZ + 1,)),
            pltpu.SemaphoreType.DMA((AT_SLOTS + 8 * NZ,)),
        ],
        compiler_params=pltpu.CompilerParams(
            collective_id=0, has_side_effects=True, vmem_limit_bytes=56 * 1024 * 1024
        ),
        name="video_attention",
    )(*operands)


def solution(mesh):
    placed = (
        P("blk", "uly", None),
        P(),
        P(None, "uly"),
        P("blk", "uly"),
        P("blk", None),
        P("uly"),
        P("uly", None),
        P("uly", None),
        P("uly", None),
        P(),
        P(),
        P(),
    )
    return jax.shard_map(
        shards, mesh=mesh, in_specs=placed, out_specs=P("blk", "uly"), check_vma=False
    )
```

time: 233 us -> 142 us (0.61)
  Pallas kernels: 88.5 us -> 139 us
  blocking collectives: 48 us -> 0 us
  waiting for transfers between devices: 47.7 us -> 0 us
  other arithmetic: 15.1 us -> 0 us
  local copies, waits for them, and re-layouts: 15.1 us -> 3.06 us
  starting transfers between devices: 9.9 us -> 0 us
  matrix products: 7.24 us -> 0 us
    pallas_call x1, Pallas kernels: 88.5 us -> 139 us  [shards(): pl.pallas_call(kernel, out_shape=jax.ShapeDtypeStruct((GRP, 2 * HD), bf16...]
    all_to_all x1 -> x0, waiting for transfers between devices: 47.7 us -> none  [shards(): lax.all_to_all(partials, 'uly', split_axis=0, concat_axis=0, tiled=True)]
    all_gather x1 -> x0, blocking collectives: 29.5 us -> none  [shards(): lax.all_gather(normal_vis, 'uly', axis=1, tiled=True)]
    psum x1 -> x0, blocking collectives: 18.5 us -> none  [shards(): row_sums = lax.psum(jnp.sum(seq_float * seq_float, 1), 'uly')]
    dot_general x2 -> x0, matrix products: 7.24 us -> none  [the longest x1 6.72 us: shards(): jnp.einsum('wt,tai->awi', normalized_rows, slot_weight_matrix, preferred_...]
    gather x2 -> x0, local copies, waits for them, and re-layouts: 5.36 us -> none  [the longest x1 2.68 us: alternate(): jnp.take(vis_rows, vis_index, 0)]
    reduce_sum x6 -> x0, other arithmetic: 5.07 us -> none  [the longest x1 3.09 us: shards(): projected = jnp.sum(received.astype(jnp.float32), 0) + slot_bias]
    ppermute x1 -> x0, starting transfers between devices: 4.97 us -> none  [from_behind(): lax.ppermute(value, axis, [(source, source + steps) for source in range(f...]
  transfers between devices with their start and end apart: 2 -> 0, of which waited for: 1 -> 0; matrix products, arithmetic and copies ran while one was open for 5% -> 0% of each run, Pallas kernels for 0% -> 0%
where the time goes in v3:
time: 142 us
  Pallas kernels  139 us (98%)
  local copies, waits for them, and re-layouts  3.06 us (2%)
    pallas_call x1, Pallas kernels, shards(): pl.pallas_call(kernel, out_shape=jax.ShapeDtypeStruct((GRP, 2 * HD), bf16...  139 us

profile of v3, /device:TPU:224, one launch (start us, length us, event | category | flops | bytes accessed | tf_op | source)
XLA Modules:
  0.0 141.7 jit_solution(9836163392755922077)
XLA Ops:
  0.0 1.3 broadcast_in_dim.15.vis_gain_hbm
  1.3 138.6 %video_attention.1 = bf16[768,256]{1,0:T(8,128)(2,1)} custom-call(bf16[8,8,1152]{2,1,0:T(8,128)(2,1)} %frames_hbm.1, f32[1,1152]{1,0:T(1,128)} %broadcast_in_dim.15.vis_gain_hbm, bf16[448,1152]{1,0:T(8,128)(2,1)} %bitcast.6, bf16[448,512]{1,0:T(8,128)(2,1)} %bitcast.7, s32[1,5]{1,0:T(1,128)} %lengths_hbm.1, f32[1,448]{1,0:T(1,128)} %bitcast.9, ...), custom_call_target="tpu_custom_call" | custom-call | tf_op jit(solution)/shard_map/video_attention/pallas_call | solution.py:646
  139.9 1.8 %copy.15 = bf16[768,256]{1,0:T(8,128)(2,1)} copy(bf16[768,256]{1,0:T(8,128)(2,1)} %video_attention.1) | data formatting | bytes 786432

commit v4 on v3

--- a/solution.py
+++ b/solution.py
@@ -31,6 +31,8 @@
 AT_HALO, AT_TEXT, AT_VIS, AT_GATHER = 0, 0, 8, 16
 AT_FAR, AT_NEAR, AT_PAIR = (24, 36), (48, 60), (72, 78)
 AT_SLOTS = 84
+
+SIDE = 256
 
 
 def kernel(
@@ -329,71 +331,103 @@
             result = jnp.dot(chosen, done[kind][...], preferred_element_type=jnp.float32)
             write(slice(chunk * CHUNK, chunk * CHUNK + CHUNK), result.astype(jnp.bfloat16))
 
-    def slot(stage, far, other):
-        return stage * 8 + far * 2 + other
-
-    def slot_copy(source, target, sem, to):
+    def piece_copy(source, target, sem, landing, to):
         return pltpu.make_async_remote_copy(
-            src_ref=slots.at[source],
-            dst_ref=slots.at[target],
+            src_ref=source,
+            dst_ref=target,
             send_sem=send_sem.at[AT_SLOTS + sem],
-            recv_sem=recv_sem.at[AT_SLOTS + target],
+            recv_sem=recv_sem.at[AT_SLOTS + landing],
             device_id=to,
             device_id_type=MESH,
         )
 
-    def send(source, target, sem, to):
-        slot_copy(source, target, sem, to).start()
-
-    def arrived(target):
-        slot_copy(target, target, target, sibling).wait_recv()
-
-    def spread(stage):
-        mine = slot(stage, 0, 0)
-        send(mine, slot(stage, 1, 0), stage * 8 + 1, y_up)
-        send(mine, slot(stage, 3, 0), stage * 8 + 2, y_down)
-        send(mine, slot(stage, 0, 1), stage * 8 + 4, sibling)
-
-    def step_z(stage):
-        arrived(slot(stage, 0, 0))
+    def front(stage, far):
+        return slots.at[stage, 0, far, SIDE:GRP]
+
+    def side(far):
+        return slots.at[0, 0, far, 0:SIDE]
+
+    def sides(stage):
+        return slots.at[stage, 0, :, 0:SIDE]
+
+    def send(source, target, sem, landing, to):
+        piece_copy(source, target, sem, landing, to).start()
+
+    def arrived(target, landing):
+        piece_copy(target, target, 0, landing, sibling).wait_recv()
+
+    def settled(source, sem):
+        piece_copy(source, source, sem, 0, sibling).wait_send()
+
+    def pass_z(stage, piece, sem, landing):
         odd = lax.rem(stage, 2) == 1
 
         @pl.when(odd & (stage + 2 < NZ))
         def _():
-            send(slot(stage, 0, 0), slot(stage + 2, 0, 0), stage * 8, z_up)
+            send(piece(stage), piece(stage + 2), sem, landing, z_up)
 
         @pl.when(jnp.logical_not(odd) & (stage + 2 < NZ))
         def _():
-            send(slot(stage, 0, 0), slot(stage + 2, 0, 0), stage * 8, z_down)
-
-        spread(stage)
+            send(piece(stage), piece(stage + 2), sem, landing, z_down)
+
+    def own_front(stage):
+        return front(stage, 0)
+
+    def to_neighbours(stage):
+        send(front(stage, 0), front(stage, 1), stage * 8 + 1, stage * 4 + 1, y_up)
+        send(front(stage, 0), front(stage, 3), stage * 8 + 2, stage * 4 + 3, y_down)
+
+    def step_start():
+        send(side(0), side(1), 66, 33, y_up)
+        send(side(0), side(3), 67, 35, y_down)
+        send(front(0, 0), front(1, 0), 0, 4, z_up)
+        send(front(0, 0), front(2, 0), 64, 8, z_down)
+        to_neighbours(0)
+
+    def step_z(stage):
+        arrived(front(stage, 0), stage * 4)
+        pass_z(stage, own_front, stage * 8, (stage + 2) * 4)
+        to_neighbours(stage)
 
     def step_y(stage):
-        arrived(slot(stage, 1, 0))
-        arrived(slot(stage, 3, 0))
+        if isinstance(stage, int) and stage == 0:
+            for far in (1, 3):
+                arrived(side(far), 32 + far)
+            send(side(1), side(2), 68, 34, y_up)
+        else:
+            arrived(sides(stage), 36 + stage)
+            pass_z(stage, sides, stage * 8 + 4, 38 + stage)
+        for far in (1, 3):
+            arrived(front(stage, far), stage * 4 + far)
         odd = lax.rem(stage, 2) == 1
 
         @pl.when(odd)
         def _():
-            send(slot(stage, 3, 0), slot(stage, 2, 0), stage * 8 + 3, y_down)
+            send(front(stage, 3), front(stage, 2), stage * 8 + 3, stage * 4 + 2, y_down)
 
         @pl.when(jnp.logical_not(odd))
         def _():
-            send(slot(stage, 1, 0), slot(stage, 2, 0), stage * 8 + 3, y_up)
-
-        send(slot(stage, 1, 0), slot(stage, 1, 1), stage * 8 + 5, sibling)
-        send(slot(stage, 3, 0), slot(stage, 3, 1), stage * 8 + 7, sibling)
+            send(front(stage, 1), front(stage, 2), stage * 8 + 3, stage * 4 + 2, y_up)
 
     def step_far(stage):
-        arrived(slot(stage, 2, 0))
-        send(slot(stage, 2, 0), slot(stage, 2, 1), stage * 8 + 6, sibling)
+        if isinstance(stage, int) and stage == 0:
+            arrived(side(2), 34)
+            send(sides(0), sides(1), 4, 37, z_up)
+            send(sides(0), sides(2), 65, 38, z_down)
+        arrived(front(stage, 2), stage * 4 + 2)
+        send(slots.at[stage, 0], slots.at[stage, 1], stage * 8 + 5, 44 + stage, sibling)
 
     def step_sibling(stage):
-        for far in range(NY):
-            arrived(slot(stage, far, 1))
+        arrived(slots.at[stage, 1], 44 + stage)
+
+    def block_of(where, count, last):
+        stage, other, far = where
+        if count == 1:
+            return slots[stage, other, far, 0:last, :]
+        return slots[stage, :, far].reshape(count * GRP, HD)
 
     def scores_of(keys, count, row, head, last):
-        block = slots[pl.ds(keys, count), 0:last, :].reshape(count * last, HD)
+        block = block_of(keys, count, last)
         return lax.dot_general(
             queries[row : row + ROWS, head * HD : (head + 1) * HD],
             block,
@@ -414,7 +448,7 @@
             old_top = top[at, :]
             new_top = jnp.maximum(old_top, block_top)
         weights = jnp.exp2(scores * EXP2_SCALE - new_top[:, :1]).astype(jnp.bfloat16)
-        block = slots[pl.ds(values, count), 0:last, :].reshape(count * last, HD)
+        block = block_of(values, count, last)
         gained = jnp.dot(
             weights,
             jnp.concatenate([block, jnp.ones(block.shape, jnp.bfloat16)], 1),
@@ -480,12 +514,10 @@
     finish(KV, 5)
 
     def write_piece(at, result):
-        slots[0, at, :] = result
+        slots[0, 0, 0, at, :] = result
 
     ordered(KV, write_piece)
-    send(0, slot(1, 0, 0), 0, z_up)
-    send(0, slot(2, 0, 0), 64, z_down)
-    spread(0)
+    step_start()
 
     send_far(Q, 4)
     send_far(Q, 5)
@@ -520,7 +552,7 @@
     step_z(5)
 
     own_pair = 1 + 2 * (1 - y_lo)
-    unit(slot(0, y_lo * own_pair, 0), slot(0, (1 - y_lo) * own_pair, 0), 1, True)
+    unit((0, 0, y_lo * own_pair), (0, 0, (1 - y_lo) * own_pair), 1, True)
     step_sibling(0)
 
     def stage_zero(part, carry):
@@ -529,8 +561,8 @@
             part_hi, part_core = lax.div(part, 2), lax.rem(part, 2)
             other = lax.rem(part_core + core, 2)
             unit(
-                slot(0, lax.rem(y - 2 * part_hi + NY, NY), other),
-                slot(0, lax.rem(y - 2 * part_hi - 1 + NY, NY), other),
+                (0, other, lax.rem(y - 2 * part_hi + NY, NY)),
+                (0, other, lax.rem(y - 2 * part_hi - 1 + NY, NY)),
                 1,
                 False,
             )
@@ -565,8 +597,8 @@
         @pl.when(from_z >= 0)
         def _():
             unit(
-                slot(stage, lax.rem(y - 2 * part_hi + NY, NY), 0),
-                slot(stage, lax.rem(y - 2 * part_hi - 1 + NY, NY), 0),
+                (stage, 0, lax.rem(y - 2 * part_hi + NY, NY)),
+                (stage, 0, lax.rem(y - 2 * part_hi - 1 + NY, NY)),
                 2,
                 False,
             )
@@ -584,18 +616,24 @@
 
     for each in copies:
         each.wait_send()
-    slot_copy(0, 0, 64, sibling).wait_send()
-
-    def settle(index, carry):
-        stage, kind = lax.div(index, 8), lax.rem(index, 8)
-
-        @pl.when((kind > 0) | (stage + 2 < NZ))
+    settled(front(0, 0), 64)
+    settled(sides(0), 65)
+    for step in range(3):
+        settled(side(0), 66 + step)
+
+    def settle(stage, carry):
+        for kind in range(1, 4):
+            settled(front(0, 0), stage * 8 + kind)
+        settled(slots.at[0, 0], stage * 8 + 5)
+
+        @pl.when(stage + 2 < NZ)
         def _():
-            slot_copy(0, 0, index, sibling).wait_send()
+            settled(front(0, 0), stage * 8)
+            settled(sides(0), stage * 8 + 4)
 
         return carry
 
-    lax.fori_loop(0, 8 * NZ, settle, 0)
+    lax.fori_loop(0, NZ, settle, 0)
 
 
 def shards(
@@ -665,12 +703,12 @@
             pltpu.VMEM((GRP, HD), bf16),
             pltpu.VMEM((GRP, 2 * HD), bf16),
             pltpu.VMEM((GRP, 2 * HD), bf16),
-            pltpu.VMEM((8 * NZ, GRP, HD), bf16),
+            pltpu.VMEM((NZ, 2, NY, GRP, HD), bf16),
             pltpu.VMEM((2 * GRP, HD), f32),
             pltpu.VMEM((2 * GRP, 2 * HD), f32),
             pltpu.SemaphoreType.DMA((len(operands),)),
-            pltpu.SemaphoreType.DMA((AT_SLOTS + 8 * NZ + 1,)),
-            pltpu.SemaphoreType.DMA((AT_SLOTS + 8 * NZ,)),
+            pltpu.SemaphoreType.DMA((AT_SLOTS + 69,)),
+            pltpu.SemaphoreType.DMA((AT_SLOTS + 52,)),
         ],
         compiler_params=pltpu.CompilerParams(
             collective_id=0, has_side_effects=True, vmem_limit_bytes=56 * 1024 * 1024

time: 142 us -> 130 us (0.915)
  Pallas kernels: 139 us -> 127 us
    pallas_call x1, Pallas kernels: 139 us -> 127 us  [shards(): pl.pallas_call(kernel, out_shape=jax.ShapeDtypeStruct((GRP, 2 * HD), bf16...]
where the time goes in v4:
time: 130 us
  Pallas kernels  127 us (98%)
  local copies, waits for them, and re-layouts  3.06 us (2%)
    pallas_call x1, Pallas kernels, shards(): pl.pallas_call(kernel, out_shape=jax.ShapeDtypeStruct((GRP, 2 * HD), bf16...  127 us

profile of v4, /device:TPU:224, one launch (start us, length us, event | category | flops | bytes accessed | tf_op | source)
XLA Modules:
  0.0 129.9 jit_solution(18064262089969779270)
XLA Ops:
  0.0 1.3 broadcast_in_dim.15.vis_gain_hbm
  1.3 126.8 %video_attention.1 = bf16[768,256]{1,0:T(8,128)(2,1)} custom-call(bf16[8,8,1152]{2,1,0:T(8,128)(2,1)} %frames_hbm.1, f32[1,1152]{1,0:T(1,128)} %broadcast_in_dim.15.vis_gain_hbm, bf16[448,1152]{1,0:T(8,128)(2,1)} %bitcast.6, bf16[448,512]{1,0:T(8,128)(2,1)} %bitcast.7, s32[1,5]{1,0:T(1,128)} %lengths_hbm.1, f32[1,448]{1,0:T(1,128)} %bitcast.9, ...), custom_call_target="tpu_custom_call" | custom-call | tf_op jit(solution)/shard_map/video_attention/pallas_call | solution.py:684
  128.1 1.8 %copy.15 = bf16[768,256]{1,0:T(8,128)(2,1)} copy(bf16[768,256]{1,0:T(8,128)(2,1)} %video_attention.1) | data formatting | bytes 786432

commit v5 on v4

--- a/solution.py
+++ b/solution.py
@@ -424,7 +424,10 @@
         stage, other, far = where
         if count == 1:
             return slots[stage, other, far, 0:last, :]
-        return slots[stage, :, far].reshape(count * GRP, HD)
+        beyond = lax.rem(far + 2, NY)
+        return jnp.concatenate(
+            [slots[stage, :, at].reshape(2 * GRP, HD) for at in (far, beyond)], 0
+        )
 
     def scores_of(keys, count, row, head, last):
         block = block_of(keys, count, last)
@@ -571,24 +574,20 @@
 
     lax.fori_loop(0, 3, stage_zero, 0)
 
-    def later_stages(index, carry):
-        stage, part_hi = lax.div(index, 2), lax.rem(index, 2)
-
-        @pl.when(part_hi == 0)
-        def _():
-            @pl.when(stage + 5 < NZ)
-            def _():
-                step_z(stage + 5)
-
-            @pl.when(stage + 3 < NZ)
-            def _():
-                step_y(stage + 3)
-
-            @pl.when(stage + 2 < NZ)
-            def _():
-                step_far(stage + 2)
-
-            step_sibling(stage)
+    def later_stages(stage, carry):
+        @pl.when(stage + 5 < NZ)
+        def _():
+            step_z(stage + 5)
+
+        @pl.when(stage + 3 < NZ)
+        def _():
+            step_y(stage + 3)
+
+        @pl.when(stage + 2 < NZ)
+        def _():
+            step_far(stage + 2)
+
+        step_sibling(stage)
 
         hops = lax.div(stage + 1, 2)
         odd = lax.rem(stage, 2)
@@ -596,16 +595,11 @@
 
         @pl.when(from_z >= 0)
         def _():
-            unit(
-                (stage, 0, lax.rem(y - 2 * part_hi + NY, NY)),
-                (stage, 0, lax.rem(y - 2 * part_hi - 1 + NY, NY)),
-                2,
-                False,
-            )
+            unit((stage, 0, y), (stage, 0, lax.rem(y + NY - 1, NY)), 4, False)
 
         return carry
 
-    lax.fori_loop(2, 2 * NZ, later_stages, 0)
+    lax.fori_loop(1, NZ, later_stages, 0)
 
     for row in range(0, GRP, ROWS):
         for head in range(2):

time: 130 us -> 127 us (0.977)
  Pallas kernels: 127 us -> 123 us
    pallas_call x1, Pallas kernels: 127 us -> 123 us  [shards(): pl.pallas_call(kernel, out_shape=jax.ShapeDtypeStruct((GRP, 2 * HD), bf16...]
where the time goes in v5:
time: 127 us; the launch traced here: 126 us
  Pallas kernels  123 us (97%)
  local copies, waits for them, and re-layouts  3.06 us (2%)
    pallas_call x1, Pallas kernels, shards(): pl.pallas_call(kernel, out_shape=jax.ShapeDtypeStruct((GRP, 2 * HD), bf16...  123 us

profile of v5, /device:TPU:224, one launch (start us, length us, event | category | flops | bytes accessed | tf_op | source)
XLA Modules:
  0.0 126.4 jit_solution(15752127938051699886)
XLA Ops:
  0.0 1.3 %broadcast_in_dim.15.vis_gain_hbm = f32[1,1152]{1,0:T(1,128)} reshape(f32[1152]{0:T(1024)} %param.14) | data formatting | bytes 9216 | tf_op jit(solution)/shard_map/broadcast_in_dim | solution.py:651
  1.3 123.3 %video_attention.1 = bf16[768,256]{1,0:T(8,128)(2,1)} custom-call(bf16[8,8,1152]{2,1,0:T(8,128)(2,1)} %frames_hbm.1, f32[1,1152]{1,0:T(1,128)} %broadcast_in_dim.15.vis_gain_hbm, bf16[448,1152]{1,0:T(8,128)(2,1)} %bitcast.6, bf16[448,512]{1,0:T(8,128)(2,1)} %bitcast.7, s32[1,5]{1,0:T(1,128)} %lengths_hbm.1, f32[1,448]{1,0:T(1,128)} %bitcast.9, ...), custom_call_target="tpu_custom_call" | custom-call | tf_op jit(solution)/shard_map/video_attention/pallas_call | solution.py:678
  124.6 1.8 %copy.15 = bf16[768,256]{1,0:T(8,128)(2,1)} copy(bf16[768,256]{1,0:T(8,128)(2,1)} %video_attention.1) | data formatting | bytes 786432
